TPU v7x, 512 devices: a whole 4x4x16 slice. The times are simulated.
512 devices in a mesh: stream: 64 (over x, z), cross: 8 (over y, core).
Axes of the slice: x: 4, y: 4, z: 16, core: 2. Of those that a mesh axis runs over, the one named last changes fastest.
Arguments:
- source: float32 [512, 64, 128], P('stream', 'cross'), may hold values from -6 to 6
- metric: float32 [64, 8, 16], P('stream', 'cross'), may hold values from 0.5 to 4
- base_velocity: float32 [3, 512, 64, 128], P(None, 'stream', 'cross'), may hold values from -6 to 6
- drop_elem: int32 [64, 8, 5, 128], P('stream', 'cross'), may hold values from 0 to 8191, as said below
- drop_coord: float32 [64, 8, 5, 3, 128], P('stream', 'cross'), may hold values from -1 to 1
- drop_vel: float32 [64, 8, 5, 3, 128], P('stream', 'cross'), may hold values from -6 to 6
- drop_prop: float32 [64, 8, 5, 2, 128], P('stream', 'cross'), may hold values from 0.5 to 4
- drop_counts: int32 [64, 8, 5], P('stream', 'cross'), may hold values from 0 to 128, as said below
Outputs:
- pressure: float32 [512, 64, 128], P('stream', 'cross')
- momentum_source: float32 [3, 512, 64, 128], P(None, 'stream', 'cross')
- drop_accel: float32 [64, 8, 5, 3, 128], P('stream', 'cross')
Inputs may be any that keep to these rules, and one draw needn't show every extreme that they name: `drop_elem`: elements are numbered (ex * 8 + ey) * 16 + ez. The owner element of every slot of block b of holder (s, c) lies in slab s + b - 2 (streamwise element index from (s + b - 2) * 1 to that plus 1 - 1) and column c (element index from c * 1 to c + 1 - 1); this holds for slots that are not live as well, for blocks whose slab lies in the grid. `drop_counts`: A block whose owner slab s + b - 2 lies outside 0 to 63 has count 0. In every draw some slab of some column receives 128 live droplets from each of its 5 holder slabs.
All inputs are finite; a program needn't handle non-finite values.
Results may differ from a plain program's by a relative error of at most 0.0003.
Values sent between devices are 32-bit elements; how exact they have to be, the bound alone decides.
A program may use at most 64 MiB of HBM per device.

v0:
```python
import functools

import jax
import jax.numpy as jnp
import numpy as np
from jax import lax
from jax.experimental import pallas as pl
from jax.experimental.pallas import tpu as pltpu
from jax.sharding import PartitionSpec as P

SWEEPS = 3
UPPER_BOUND = 2.5
LOWER_BOUND = UPPER_BOUND / 30.0
REACH = 5
DRIFT = 2
CAP = 128
EZ = 16
GLL_POINTS = [
    -1.0,
    -0.8717401485096066,
    -0.5917001814331423,
    -0.2092992179024789,
    0.2092992179024789,
    0.5917001814331423,
    0.8717401485096066,
    1.0,
]
F32 = jnp.float32
BF16 = jnp.bfloat16
MESH = pl.DeviceIdType.MESH

DIRS = [(1, 0), (-1, 0), (0, 1), (0, -1), (1, 1), (1, -1), (-1, 1), (-1, -1)]
SLOT = {d: k for k, d in enumerate(DIRS)}
ORDER = [4, 5, 6, 7, 0, 1, 2, 3]


def legendre_seven(points):
    before = points * 0.0 + 1.0
    current = points
    for order in range(1, 7):
        following = ((2.0 * order + 1.0) * points * current - order * before) / (order + 1.0)
        before = current
        current = following
    return current


def gll_tables():
    nodes = np.array(GLL_POINTS)
    values = legendre_seven(nodes)
    weights = 2.0 / (56.0 * values * values)
    deriv = np.zeros((8, 8))
    for row in range(8):
        for col in range(8):
            if row != col:
                deriv[row, col] = values[row] / (values[col] * (nodes[row] - nodes[col]))
    deriv[0, 0] = -14.0
    deriv[7, 7] = 14.0
    return nodes, weights, deriv


NODES, WEIGHTS, DERIV = gll_tables()
STIFF = DERIV.T @ (WEIGHTS[:, None] * DERIV)
QDIAG = np.diag(STIFF)

T_WK, T_QK, T_KT, T_EYE, T_WJ, T_QJ, T_CY, T_DT, T_LAG, T_ZM = 0, 1, 2, 3, 4, 5, 6, 14, 22, 23
TILES = 24


def constant_tiles():
    lane = np.arange(128)
    row = np.arange(8)
    tiles = np.zeros((TILES, 8, 128))
    tiles[T_WK] = WEIGHTS[lane % 8][None, :]
    tiles[T_QK] = QDIAG[lane % 8][None, :]
    tiles[T_KT] = STIFF[lane % 8, :].T
    tiles[T_EYE] = lane[None, :] % 8 == row[:, None]
    tiles[T_WJ] = WEIGHTS[:, None]
    tiles[T_QJ] = QDIAG[:, None]
    for turn in range(8):
        tiles[T_CY + turn] = STIFF[row, (row - turn) % 8][:, None]
        tiles[T_DT + turn] = DERIV[(row - turn) % 8, row][:, None]
    gaps = NODES[:, None] - NODES[None, :] + np.eye(8)
    tiles[T_LAG] = (1.0 / gaps.prod(1))[:, None]
    last = (lane % 8 == 7) & (lane < 127)
    first = (lane % 8 == 0) & (lane > 0)
    tiles[T_ZM] = (last | first)[None, :]
    return tiles.astype(np.float32)


def iota(dim):
    return lax.broadcasted_iota(jnp.int32, (8, 128), dim)


def total(terms):
    terms = list(terms)
    while len(terms) > 1:
        pairs = [a + b for a, b in zip(terms[::2], terms[1::2])]
        if len(terms) % 2:
            pairs.append(terms[-1])
        terms = pairs
    return terms[0]


def wide(row):
    return jnp.broadcast_to(row, (8, 128))


def halves(value):
    high = value.astype(BF16)
    return high, (value - high.astype(F32)).astype(BF16)


def stiff_x(u):
    even = [u[m] + u[7 - m] for m in range(4)]
    odd = [u[m] - u[7 - m] for m in range(4)]
    out = [None] * 8
    for i in range(4):
        e = total(float((STIFF[i, m] + STIFF[i, 7 - m]) / 2.0) * even[m] for m in range(4))
        o = total(float((STIFF[i, m] - STIFF[i, 7 - m]) / 2.0) * odd[m] for m in range(4))
        out[i] = e + o
        out[7 - i] = e - o
    return out


def turned(value, tab, first):
    terms = [tab[first] * value]
    for turn in range(1, 8):
        terms.append(tab[first + turn] * pltpu.roll(value, turn, 0))
    return total(terms)


def kernel(
    src, met, bvel, elem, coord, dvel, dprop, cnt, tab,
    p_out, m_out, acc_out,
    qb, mb, bmat, lz, ld, lx, dx, ly, dy, fbase,
    hsend0, hrecv0, hsend, hrecv, fsend, frecv, dsend, drecv, rsend, rrecv,
    s0, r0, s1, r1, s4, r4, sd, rd, sr, rr,
):
    slabs, cols = lax.axis_size("stream"), lax.axis_size("cross")
    slab, col = lax.axis_index("stream"), lax.axis_index("cross")

    def device(ds, dc):
        return (lax.rem(slab + (ds + slabs), slabs), lax.rem(col + (dc + cols), cols))

    barrier = pltpu.get_barrier_semaphore()
    partners = DIRS + [(2, 0), (-2, 0)]
    for d in partners:
        pl.semaphore_signal(barrier, inc=1, device_id=device(*d), device_id_type=MESH)

    sub, lane = iota(0), iota(1)
    perm = jnp.clip(
        lane + jnp.where(lane % 8 == 7, 1, 0) - jnp.where(lane % 8 == 0, 1, 0), 0, 127
    )
    zmask = tab[T_ZM]
    wk, wj = tab[T_WK], tab[T_WJ]
    elane = lane // 8
    eperm = perm // 8

    def moved(value):
        return zmask * jnp.take_along_axis(value, perm, axis=1)

    def sum_z(value):
        return value + moved(value)

    from_x = {1: (slab > 0).astype(F32), -1: (slab < slabs - 1).astype(F32)}
    from_y = {1: (col > 0).astype(F32), -1: (col < cols - 1).astype(F32)}
    rowmask = {
        1: jnp.where(sub == 0, from_y[1], 0.0),
        -1: jnp.where(sub == 7, from_y[-1], 0.0),
    }
    edge_row = {1: 7, -1: 0}

    amet = jnp.zeros((8, 128), F32)
    for e in range(EZ):
        amet = jnp.where(elane == e, met[0, 0, e], amet)
    aw = amet * wk
    a1 = sum_z(aw)
    a23 = sum_z(amet * tab[T_QK] + wk)
    rhs = [sum_z(wk * src[i]) for i in range(8)]

    def stage(value, send, rows):
        for i in range(8):
            qb[8 * i : 8 * i + 8, :] = value[i]
        send[0, 0:8, :] = value[7]
        send[1, 0:8, :] = value[0]
        send[2, 0:8, :] = qb[pl.ds(7, 8, stride=8), :]
        send[3, 0:8, :] = qb[pl.ds(0, 8, stride=8), :]

    def tile_of(d):
        return SLOT[(d[0], 0)] if d[0] else SLOT[d]

    def copies(send, recv, send_sems, recv_sems):
        return [
            pltpu.make_async_remote_copy(
                src_ref=send.at[tile_of(DIRS[k])],
                dst_ref=recv.at[k],
                send_sem=send_sems.at[k],
                recv_sem=recv_sems.at[k],
                device_id=device(*DIRS[k]),
                device_id_type=MESH,
            )
            for k in ORDER
        ]

    def combine(value, recv, row):
        def face(side):
            full = recv(SLOT[(side, 0)])[0:8, :]
            full += rowmask[1] * row(recv(SLOT[(side, 1)]), 7)
            full += rowmask[-1] * row(recv(SLOT[(side, -1)]), 0)
            return from_x[side] * full

        out = []
        for i in range(8):
            terms = [value[i]]
            terms.append(rowmask[1] * row(recv(SLOT[(0, 1)]), i))
            terms.append(rowmask[-1] * row(recv(SLOT[(0, -1)]), i))
            if i == 0:
                terms.append(face(1))
            if i == 7:
                terms.append(face(-1))
            out.append(total(terms))
        return out

    def row_of(ref, i):
        return wide(ref[i : i + 1, :])

    stage(rhs, hsend0, 8)
    rows = jnp.where(sub == 0, a1, a23)
    for k in range(4):
        hsend0[k, 8:16, :] = rows

    for b in range(REACH):
        dsend[b, 0:3, :] = coord[b]
        dsend[b, 3:6, :] = dvel[b]
        dsend[b, 6:7, :] = dprop[b, 0:1, :] * dprop[b, 1:2, :]
        dsend[b, 7:8, :] = jnp.where(
            lane[0:1] < cnt[0, 0, b], (elem[b] % EZ).astype(F32), -1.0
        )

    def drop_copy(b):
        return pltpu.make_async_remote_copy(
            src_ref=dsend.at[b],
            dst_ref=drecv.at[b],
            send_sem=sd.at[b],
            recv_sem=rd.at[b],
            device_id=device(b - DRIFT, 0),
            device_id_type=MESH,
        )

    def back_copy(b):
        return pltpu.make_async_remote_copy(
            src_ref=rsend.at[b],
            dst_ref=rrecv.at[b],
            send_sem=sr.at[b],
            recv_sem=rr.at[b],
            device_id=device(DRIFT - b, 0),
            device_id_type=MESH,
        )

    away = [0, 4, 1, 3]

    pl.semaphore_wait(barrier, len(partners))
    flight0 = copies(hsend0, hrecv0, s0, r0)
    for copy in flight0:
        copy.start()
    drops = [drop_copy(b) for b in away]
    for copy in drops:
        copy.start()

    t8 = tab[T_KT] * amet + tab[T_EYE] * wk
    g8 = moved(t8)
    bfull = jnp.concatenate(
        [
            jnp.where(elane == e, t8, 0.0) + jnp.where(eperm == e, g8, 0.0)
            for e in range(EZ)
        ],
        axis=0,
    )
    bhigh, blow = halves(bfull)
    bmat[0:128, 0:128] = bhigh
    bmat[0:128, 128:256] = blow
    bmat[128:256, 0:128] = bhigh
    bmat[128:256, 128:256] = jnp.zeros((128, 128), BF16)

    def operator(u):
        high, low = halves(jnp.concatenate(u, axis=0))
        both = jnp.dot(
            jnp.concatenate([high, low], axis=1), bmat[...], preferred_element_type=F32
        )
        along_z = both[:, 0:128] + both[:, 128:256]
        along_x = stiff_x(u)
        out = []
        for i in range(8):
            along_y = turned(u[i], tab, T_CY)
            plane = (wj * along_x[i] + float(WEIGHTS[i]) * along_y) * aw
            first = (float(WEIGHTS[i]) * wj) * along_z[8 * i : 8 * i + 8, :]
            out.append(first + sum_z(plane))
        return out

    def basis_block(b):
        def basis(r):
            value = tab[T_LAG]
            for m in range(8):
                value = value * jnp.where(sub == m, 1.0, r - float(NODES[m]))
            return value, turned(value, tab, T_DT)

        tile = drecv.at[b] if b != DRIFT else dsend.at[b]
        eid = row_of(tile, 7)
        lx[b], dx[b] = basis(row_of(tile, 0))
        ly[b], dy[b] = basis(row_of(tile, 1))
        span = slice(b * CAP, b * CAP + CAP)
        for part, ref in zip(basis(row_of(tile, 2)), (lz, ld)):
            high = part.astype(BF16).astype(F32)
            for piece, start in ((high, 0), (part - high, 128)):
                spread = jnp.concatenate(
                    [jnp.where(eid == float(e), piece, 0.0) for e in range(EZ)], axis=0
                )
                ref[start : start + 128, span] = spread.astype(BF16)

    def contract(planes, span, first, second):
        inner = total(row_of(first, i) * planes[i][:, span] for i in range(8))
        return jnp.sum(second[...] * inner, axis=0, keepdims=True)

    def base_values():
        flat = jnp.concatenate([bvel[c, i] for c in range(3) for i in range(8)], axis=0)
        high, low = halves(flat)
        left = jnp.concatenate(
            [
                jnp.concatenate([high, high], axis=1),
                jnp.concatenate([low, jnp.zeros_like(low)], axis=1),
            ],
            axis=0,
        )
        for b in range(REACH):
            span = slice(b * CAP, b * CAP + CAP)
            both = jnp.dot(left, lz[:, span], preferred_element_type=F32)
            both = both[0:192, :] + both[192:384, :]
            for c in range(3):
                planes = [both[64 * c + 8 * i : 64 * c + 8 * i + 8, :] for i in range(8)]
                fbase[b, c : c + 1, :] = contract(planes, slice(0, 128), lx.at[b], ly.at[b])

    basis_block(DRIFT)

    for copy in flight0:
        copy.wait_recv()
    residual = combine(rhs, lambda k: hrecv0.at[k], row_of)

    def diag_rows(own, offset):
        def from_slot(d):
            return row_of(hrecv0.at[SLOT[d]], 8 + offset)

        middle = own + rowmask[1] * from_slot((0, 1)) + rowmask[-1] * from_slot((0, -1))
        ends = {}
        for side in (1, -1):
            extra = from_slot((side, 0))
            extra += rowmask[1] * from_slot((side, 1)) + rowmask[-1] * from_slot((side, -1))
            ends[side] = middle + from_x[side] * extra
        return [ends[1]] + [middle] * 6 + [ends[-1]]

    center = (UPPER_BOUND + LOWER_BOUND) / 2.0
    half_width = (UPPER_BOUND - LOWER_BOUND) / 2.0
    bound = center / half_width
    rho = 1.0 / bound

    a1_all, a23_all = diag_rows(a1, 0), diag_rows(a23, 1)
    inv_diag, update = [], []
    for i in range(8):
        w_i, q_i = float(WEIGHTS[i]), float(QDIAG[i])
        residual[i] = (w_i * wj) * residual[i]
        diagonal = (q_i * wj + w_i * tab[T_QJ]) * a1_all[i] + (w_i * wj) * a23_all[i]
        inv_diag.append(1.0 / diagonal)
        update.append(inv_diag[i] * residual[i] * (1.0 / center))
    iterate = update

    flights = []
    for sweep in range(SWEEPS):
        local = operator(update)
        stage(local, hsend.at[sweep], 8)
        flight = copies(hsend.at[sweep], hrecv.at[sweep], s1.at[sweep], r1.at[sweep])
        for copy in flight:
            copy.start()
        flights.append(flight)
        if sweep == 0:
            for copy in drops:
                copy.wait_recv()
            basis_block(1)
            basis_block(3)
        elif sweep == 1:
            basis_block(0)
            basis_block(4)
        elif sweep == 2:
            base_values()
        for copy in flight:
            copy.wait_recv()
        step = combine(local, lambda k: hrecv.at[sweep, k], row_of)
        rho_next = 1.0 / (2.0 * bound - rho)
        for i in range(8):
            residual[i] = residual[i] - step[i]
        update = [
            (rho_next * rho) * update[i]
            + (2.0 * rho_next / half_width) * (inv_diag[i] * residual[i])
            for i in range(8)
        ]
        rho = rho_next
        iterate = [iterate[i] + update[i] for i in range(8)]

    for i in range(8):
        p_out[i] = iterate[i]

    scaled = jnp.concatenate([amet * iterate[i] for i in range(8)], axis=0)
    high, low = halves(scaled)
    left = jnp.concatenate(
        [
            jnp.concatenate([high, high], axis=1),
            jnp.concatenate([low, jnp.zeros_like(low)], axis=1),
        ],
        axis=0,
    )
    forces = []
    for b in range(REACH):
        span = slice(b * CAP, b * CAP + CAP)
        whole = slice(0, 128)

        def planes_of(ref):
            both = jnp.dot(left, ref[:, span], preferred_element_type=F32)
            both = both[0:64, :] + both[64:128, :]
            return [both[8 * i : 8 * i + 8, :] for i in range(8)]

        flat, slope = planes_of(lz), planes_of(ld)
        grads = [
            contract(flat, whole, dx.at[b], ly.at[b]),
            contract(flat, whole, lx.at[b], dy.at[b]),
            contract(slope, whole, lx.at[b], ly.at[b]),
        ]
        tile = drecv.at[b] if b != DRIFT else dsend.at[b]
        force = []
        for c in range(3):
            fluid = fbase[b, c : c + 1, :] - grads[c]
            rsend[b, c : c + 1, :] = fluid
            force.append(tile[6:7, :] * (tile[3 + c : 4 + c, :] - fluid))
        forces.append(force)
    backs = [back_copy(b) for b in away]
    for copy in backs:
        copy.start()

    columns_high, columns_low = [], []
    for b in range(REACH):
        rows_ = []
        for c in range(3):
            weighted = wide(forces[b][c]) * ly[b]
            rows_ += [weighted * row_of(lx.at[b], i) for i in range(8)]
        high, low = halves(jnp.concatenate(rows_, axis=0))
        columns_high.append(high)
        columns_low.append(low)
    left = jnp.concatenate(
        [jnp.concatenate(columns_high, axis=1), jnp.concatenate(columns_low, axis=1)], axis=0
    )
    both = lax.dot_general(
        left, lz[...], (((1,), (1,)), ((), ())), preferred_element_type=F32
    )
    drag = both[0:192, 0:128] + both[0:192, 128:256] + both[192:384, 0:128]
    drag = [sum_z(drag[8 * i : 8 * i + 8, :]) for i in range(24)]
    for i in range(24):
        mb[8 * i : 8 * i + 8, :] = drag[i]
    for c in range(3):
        fsend[0, c] = drag[8 * c + 7]
        fsend[1, c] = drag[8 * c]
        fsend[2, c] = mb[pl.ds(64 * c + 7, 8, stride=8), :]
        fsend[3, c] = mb[pl.ds(64 * c, 8, stride=8), :]
    flight4 = copies(fsend, frecv, s4, r4)
    for copy in flight4:
        copy.start()

    for copy in backs:
        copy.wait_recv()
    for b in range(REACH):
        tile = rrecv.at[b] if b != DRIFT else rsend.at[b]
        accel = dprop[b, 0:1, :] * (tile[0:3, :] - dvel[b])
        acc_out[b] = jnp.where(iota(1)[0:3] < cnt[0, 0, b], accel, 0.0)

    for copy in flight4:
        copy.wait_recv()
    for c in range(3):
        value = combine(drag[8 * c : 8 * c + 8], lambda k: frecv.at[k, c], row_of)
        for i in range(8):
            m_out[c, i] = value[i]

    for copy in flight0 + drops + flights[0] + flights[1] + flights[2] + backs + flight4:
        copy.wait_send()


def on_device(source, metric, base, elem, coord, dvel, dprop, counts):
    vmem = pl.BlockSpec(memory_space=pltpu.VMEM)
    smem = pl.BlockSpec(memory_space=pltpu.SMEM)
    dma = pltpu.SemaphoreType.DMA
    elem = elem.reshape(REACH, 1, CAP)
    coord = coord.reshape(REACH, 3, CAP)
    dvel = dvel.reshape(REACH, 3, CAP)
    dprop = dprop.reshape(REACH, 2, CAP)
    tile = (8, 128)
    outs = pl.pallas_call(
        kernel,
        out_shape=(
            jax.ShapeDtypeStruct((8, 8, 128), F32),
            jax.ShapeDtypeStruct((3, 8, 8, 128), F32),
            jax.ShapeDtypeStruct((REACH, 3, CAP), F32),
        ),
        in_specs=[vmem, smem, vmem, vmem, vmem, vmem, vmem, smem, vmem],
        out_specs=(vmem, vmem, vmem),
        scratch_shapes=[
            pltpu.VMEM((64, 128), F32),
            pltpu.VMEM((192, 128), F32),
            pltpu.VMEM((256, 256), BF16),
            pltpu.VMEM((256, REACH * CAP), BF16),
            pltpu.VMEM((256, REACH * CAP), BF16),
            pltpu.VMEM((REACH,) + tile, F32),
            pltpu.VMEM((REACH,) + tile, F32),
            pltpu.VMEM((REACH,) + tile, F32),
            pltpu.VMEM((REACH,) + tile, F32),
            pltpu.VMEM((REACH,) + tile, F32),
            pltpu.VMEM((4, 16, 128), F32),
            pltpu.VMEM((8, 16, 128), F32),
            pltpu.VMEM((SWEEPS, 4) + tile, F32),
            pltpu.VMEM((SWEEPS, 8) + tile, F32),
            pltpu.VMEM((4, 3) + tile, F32),
            pltpu.VMEM((8, 3) + tile, F32),
            pltpu.VMEM((REACH,) + tile, F32),
            pltpu.VMEM((REACH,) + tile, F32),
            pltpu.VMEM((REACH,) + tile, F32),
            pltpu.VMEM((REACH,) + tile, F32),
            dma((8,)),
            dma((8,)),
            dma((SWEEPS, 8)),
            dma((SWEEPS, 8)),
            dma((8,)),
            dma((8,)),
            dma((REACH,)),
            dma((REACH,)),
            dma((REACH,)),
            dma((REACH,)),
        ],
        compiler_params=pltpu.CompilerParams(
            collective_id=0, has_side_effects=True, vmem_limit_bytes=32 * 1024 * 1024
        ),
    )(source, metric, base, elem, coord, dvel, dprop, counts, jnp.asarray(constant_tiles()))
    pressure, momentum, accel = outs
    return pressure, momentum, accel[None, None]


def solution(mesh):
    in_specs = (
        P("stream", "cross", None),
        P("stream", "cross", None),
        P(None, "stream", "cross", None),
        P("stream", "cross", None, None),
        P("stream", "cross", None, None, None),
        P("stream", "cross", None, None, None),
        P("stream", "cross", None, None, None),
        P("stream", "cross", None),
    )
    out_specs = (
        P("stream", "cross", None),
        P(None, "stream", "cross", None),
        P("stream", "cross", None, None, None),
    )
    return jax.shard_map(
        on_device, mesh=mesh, in_specs=in_specs, out_specs=out_specs, check_vma=False
    )
```

profile of v0, /device:TPU:1, one launch (start us, length us, event | category | flops | bytes accessed | tf_op | source)
XLA Modules:
  0.0 46.6 jit_solution(6764403983795997785)
XLA Ops:
  0.6 0.0 copy-start.2
  0.6 0.0 copy-start.3
  0.7 0.7 %copy_bitcast_fusion = (f32[5,3,128]{2,1,0:T(4,128)S(1)}, f32[5,3,128]{2,1,0:T(4,128)S(1)}) fusion(f32[1,1,5,3,128]{4,1,3,2,0:T(1,128)} %param.14, f32[1,1,5,3,128]{4,1,3,2,0:T(1,128)} %param.13), kind=kLoop, calls=%fused_computation | loop fusion | bytes 30720
  1.4 0.0 copy-start.4
  1.4 0.0 copy-start.5
  1.4 0.0 copy-start.6
  1.4 0.0 copy-done.2
  1.4 0.0 copy-done.3
  1.4 0.7 %copy-done.4 = s32[1,1,5,128]{3,1,2,0:T(1,128)S(1)} copy-done((s32[1,1,5,128]{3,1,2,0:T(1,128)S(1)}, s32[1,1,5,128]{3,1,2,0:T(1,128)}, u32[]{:S(2)}) %copy-start.4) | copy-done | bytes 2584
  2.1 0.0 copy-done.5
  2.1 0.0 copy-done.6
  2.1 0.0 copy-start
  2.1 0.9 %copy-done = f32[3,8,8,128]{3,2,1,0:T(8,128)S(1)} copy-done((f32[3,8,8,128]{3,2,1,0:T(8,128)S(1)}, f32[3,8,8,128]{3,2,1,0:T(8,128)}, u32[]{:S(2)}) %copy-start) | copy-done | bytes 98328
  3.0 0.0 copy-start.1
  3.0 0.9 %copy-done.1 = f32[24,8,128]{2,1,0:T(8,128)S(1)} copy-done((f32[24,8,128]{2,1,0:T(8,128)S(1)}, f32[24,8,128]{2,1,0:T(8,128)}, u32[]{:S(2)}) %copy-start.1) | copy-done | bytes 98328
  3.9 40.9 %shard_map.112 = (f32[8,8,128]{2,1,0:T(8,128)S(1)}, f32[3,8,8,128]{3,2,1,0:T(8,128)S(1)}, f32[5,3,128]{2,1,0:T(4,128)S(1)}) custom-call(f32[8,8,128]{2,1,0:T(8,128)S(1)} %copy-done.2, f32[1,1,16]{2,1,0:T(1,128)S(1)} %copy-done.5, f32[3,8,8,128]{3,2,1,0:T(8,128)S(1)} %copy-done, s32[5,1,128]{2,1,0:T(1,128)S(1)} %bitcast.9, ...), custom_call_target="tpu_custom_call" | custom-call | tf_op jit(solution)/shard_map/pallas_call | solution.py:501
  44.7 0.6 %copy.12 = f32[1,1,5,3,128]{4,1,3,2,0:T(1,128)} copy(f32[1,1,5,3,128]{4,3,2,1,0:T(4,128)S(1)} %bitcast.7) | data formatting | bytes 15360
  45.3 0.6 %copy.19 = f32[8,8,128]{2,1,0:T(8,128)} copy(f32[8,8,128]{2,1,0:T(8,128)S(1)} %get-tuple-element.17) | data formatting | bytes 65536
  45.9 0.6 %copy.20 = f32[3,8,8,128]{3,2,1,0:T(8,128)} copy(f32[3,8,8,128]{3,2,1,0:T(8,128)S(1)} %get-tuple-element.18) | data formatting | bytes 196608
Async XLA Ops:
  0.6 0.8 %copy-start.2 = (f32[8,8,128]{2,1,0:T(8,128)S(1)}, f32[8,8,128]{2,1,0:T(8,128)}, u32[]{:S(2)}) copy-start(f32[8,8,128]{2,1,0:T(8,128)} %src.1) | copy-start | bytes 98308
  0.6 0.8 %copy-start.3 = (f32[1,1,5,2,128]{4,3,2,1,0:T(2,128)S(1)}, f32[1,1,5,2,128]{4,3,2,1,0:T(2,128)}, u32[]{:S(2)}) copy-start(f32[1,1,5,2,128]{4,3,2,1,0:T(2,128)} %param.15) | copy-start | bytes 15364
  1.4 0.7 %copy-start.4 = (s32[1,1,5,128]{3,1,2,0:T(1,128)S(1)}, s32[1,1,5,128]{3,1,2,0:T(1,128)}, u32[]{:S(2)}) copy-start(s32[1,1,5,128]{3,1,2,0:T(1,128)} %param.12) | copy-start | bytes 7684
  1.4 0.7 %copy-start.5 = (f32[1,1,16]{2,1,0:T(1,128)S(1)}, f32[1,1,16]{2,1,0:T(1,128)}, u32[]{:S(2)}) copy-start(f32[1,1,16]{2,1,0:T(1,128)} %met.1) | copy-start | bytes 196
  1.4 0.7 %copy-start.6 = (s32[1,1,5]{2,1,0:T(1,128)S(1)}, s32[1,1,5]{2,1,0:T(1,128)}, u32[]{:S(2)}) copy-start(s32[1,1,5]{2,1,0:T(1,128)} %cnt.1) | copy-start | bytes 64
  2.1 0.9 %copy-start = (f32[3,8,8,128]{3,2,1,0:T(8,128)S(1)}, f32[3,8,8,128]{3,2,1,0:T(8,128)}, u32[]{:S(2)}) copy-start(f32[3,8,8,128]{3,2,1,0:T(8,128)} %bvel.1) | copy-start | bytes 294916
  3.0 0.9 %copy-start.1 = (f32[24,8,128]{2,1,0:T(8,128)S(1)}, f32[24,8,128]{2,1,0:T(8,128)}, u32[]{:S(2)}) copy-start(f32[24,8,128]{2,1,0:T(8,128)} %constant.2.clone.tab) | copy-start | bytes 294916
where the time goes:
time: 46.9 us; the launch traced here: 46.6 us
  Pallas kernels  40.9 us (87%)
  local copies, waits for them, and re-layouts  5.04 us (11%)
  between operations  0.68 us (1%)
    pallas_call x1, Pallas kernels, on_device(): pl.pallas_call(kernel, out_shape=(jax.ShapeDtypeStruct((8, 8, 128), F32),...  40.9 us
    unnamed x18, local copies, waits for them, and re-layouts  5.04 us

commit v1 on v0

v1 whole, which is shorter than its diff:
```python
import functools

import jax
import jax.numpy as jnp
import numpy as np
from jax import lax
from jax.experimental import pallas as pl
from jax.experimental.pallas import tpu as pltpu
from jax.sharding import PartitionSpec as P

SWEEPS = 3
UPPER_BOUND = 2.5
LOWER_BOUND = UPPER_BOUND / 30.0
REACH = 5
DRIFT = 2
CAP = 128
EZ = 16
GLL_POINTS = [
    -1.0,
    -0.8717401485096066,
    -0.5917001814331423,
    -0.2092992179024789,
    0.2092992179024789,
    0.5917001814331423,
    0.8717401485096066,
    1.0,
]
F32 = jnp.float32
BF16 = jnp.bfloat16
MESH = pl.DeviceIdType.MESH

DIRS = [(1, 0), (-1, 0), (0, 1), (0, -1), (1, 1), (1, -1), (-1, 1), (-1, -1)]
SLOT = {d: k for k, d in enumerate(DIRS)}
ORDER = [4, 5, 6, 7, 0, 1, 2, 3]
AWAY = [0, 4, 1, 3]


def legendre_seven(points):
    before = points * 0.0 + 1.0
    current = points
    for order in range(1, 7):
        following = ((2.0 * order + 1.0) * points * current - order * before) / (order + 1.0)
        before = current
        current = following
    return current


def gll_tables():
    nodes = np.array(GLL_POINTS)
    values = legendre_seven(nodes)
    weights = 2.0 / (56.0 * values * values)
    deriv = np.zeros((8, 8))
    for row in range(8):
        for col in range(8):
            if row != col:
                deriv[row, col] = values[row] / (values[col] * (nodes[row] - nodes[col]))
    deriv[0, 0] = -14.0
    deriv[7, 7] = 14.0
    return nodes, weights, deriv


NODES, WEIGHTS, DERIV = gll_tables()
STIFF = DERIV.T @ (WEIGHTS[:, None] * DERIV)
QDIAG = np.diag(STIFF)

PACKED = 5
T_WK, T_QK, T_KT, T_ZM, T_WJ, T_QJ, T_CY, T_DT, T_LAG = 0, 1, 2, 3, 4, 5, 6, 14, 22
TILES = 23


def constant_tiles():
    lane = np.arange(128)
    row = np.arange(8)
    tiles = np.zeros((PACKED, 8, 128))
    tiles[T_WK] = WEIGHTS[lane % 8][None, :]
    tiles[T_QK] = QDIAG[lane % 8][None, :]
    tiles[T_KT] = STIFF[lane % 8, :].T
    last = (lane % 8 == 7) & (lane < 127)
    first = (lane % 8 == 0) & (lane > 0)
    tiles[T_ZM] = (last | first)[None, :]
    columns = tiles[PACKED - 1]
    columns[:, T_WJ] = WEIGHTS
    columns[:, T_QJ] = QDIAG
    for turn in range(8):
        columns[:, T_CY + turn] = STIFF[row, (row - turn) % 8]
        columns[:, T_DT + turn] = DERIV[(row - turn) % 8, row]
    gaps = NODES[:, None] - NODES[None, :] + np.eye(8)
    columns[:, T_LAG] = 1.0 / gaps.prod(1)
    return tiles.astype(np.float32)


def iota(dim):
    return lax.broadcasted_iota(jnp.int32, (8, 128), dim)


def total(terms):
    terms = list(terms)
    while len(terms) > 1:
        pairs = [a + b for a, b in zip(terms[::2], terms[1::2])]
        if len(terms) % 2:
            pairs.append(terms[-1])
        terms = pairs
    return terms[0]


def wide(row):
    return jnp.broadcast_to(row, (8, 128))


def halves(value):
    high = value.astype(BF16)
    return high, (value - high.astype(F32)).astype(BF16)


def stiff_x(u):
    even = [u[m] + u[7 - m] for m in range(4)]
    odd = [u[m] - u[7 - m] for m in range(4)]
    out = [None] * 8
    for i in range(4):
        e = total(float((STIFF[i, m] + STIFF[i, 7 - m]) / 2.0) * even[m] for m in range(4))
        o = total(float((STIFF[i, m] - STIFF[i, 7 - m]) / 2.0) * odd[m] for m in range(4))
        out[i] = e + o
        out[7 - i] = e - o
    return out


def turned(value, tab, first):
    terms = [tab[first] * value]
    for turn in range(1, 8):
        terms.append(tab[first + turn] * pltpu.roll(value, turn, 0))
    return total(terms)


def kernel(
    src_h, met_h, bvel_h, elem_h, coord_h, dvel_h, dprop_h, cnt_h, tab_h,
    p_out, m_out, acc_out,
    src, met, bvel, elem, coord, dvel, dprop, cnt, pack, tab,
    ub, mb, kz, lz, ld, lx, dx, ly, dy, fbase,
    hsend, hrecv, nsend, nrecv, fsend, frecv, dsend, drecv, rsend, rrecv,
    si, s0, r0, s1, r1, s4, r4, sd, rd, sr, rr,
):
    slabs, cols = lax.axis_size("stream"), lax.axis_size("cross")
    slab, col = lax.axis_index("stream"), lax.axis_index("cross")

    loads = [
        pltpu.make_async_copy(far, near, si.at[n])
        for n, (far, near) in enumerate(
            [
                (tab_h, pack), (met_h, met), (src_h, src), (cnt_h, cnt), (elem_h, elem),
                (coord_h, coord), (dvel_h, dvel), (dprop_h, dprop), (bvel_h, bvel),
            ]
        )
    ]
    for load in loads:
        load.start()

    def device(ds, dc):
        return (slab + ds, col + dc)

    def exists(ds, dc):
        found = (slab + ds >= 0) & (slab + ds < slabs)
        return found & (col + dc >= 0) & (col + dc < cols)

    def each(copies, act):
        for copy, there in copies:
            pl.when(there)(functools.partial(act, copy))

    def start(copy):
        copy.start()

    def wait_recv(copy):
        copy.wait_recv()

    def wait_send(copy):
        copy.wait_send()

    inside = (slab >= DRIFT) & (slab < slabs - DRIFT) & (col > 0) & (col < cols - 1)

    @pl.when(jnp.logical_not(inside))
    def _():
        for ref in (hrecv, nrecv, frecv, drecv, rrecv):
            ref[...] = jnp.zeros_like(ref)

    barrier = pltpu.get_barrier_semaphore()
    partners = DIRS + [(2, 0), (-2, 0)]
    greeted = jnp.int32(0)
    for d in partners:
        there = exists(*d)
        greeted += there.astype(jnp.int32)

        @pl.when(there)
        def _():
            pl.semaphore_signal(barrier, inc=1, device_id=device(*d), device_id_type=MESH)

    sub, lane = iota(0), iota(1)
    perm = jnp.clip(
        lane + jnp.where(lane % 8 == 7, 1, 0) - jnp.where(lane % 8 == 0, 1, 0), 0, 127
    )
    elane = lane // 8
    top, bottom = sub == 0, sub == 7

    loads[0].wait()
    tab[0:4] = pack[0:4]
    columns = pack[PACKED - 1]
    for t in range(T_WJ, TILES):
        tab[t] = wide(columns[:, t : t + 1])
    wk, wj = pack[T_WK], tab[T_WJ]

    def sum_z(value):
        return value + tab[T_ZM] * jnp.take_along_axis(value, perm, axis=1)

    def edges(low, high):
        return jnp.where(top, low, jnp.where(bottom, high, 0.0))

    def row_of(ref, i):
        return wide(ref[i : i + 1, :])

    loads[1].wait()
    amet = jnp.zeros((8, 128), F32)
    for e in range(EZ):
        amet = jnp.where(elane == e, met[0, 0, e], amet)
    loads[2].wait()
    rhs = [sum_z(wk * src[i]) for i in range(8)]

    for i in range(8):
        ub[8 * i : 8 * i + 8, :] = rhs[i]
    hsend[0, 0:8, :] = rhs[7]
    hsend[1, 0:8, :] = rhs[0]
    hsend[2, 0:8, :] = ub[pl.ds(7, 8, stride=8), :]
    hsend[3, 0:8, :] = ub[pl.ds(0, 8, stride=8), :]
    for k in range(4):
        hsend[k, 8:16, :] = amet

    def tile_of(d):
        return SLOT[(d[0], 0)] if d[0] else SLOT[d]

    def copies(send, recv, send_sems, recv_sems, order):
        sent = [
            pltpu.make_async_remote_copy(
                src_ref=send.at[tile_of(DIRS[k])],
                dst_ref=recv.at[k],
                send_sem=send_sems.at[k],
                recv_sem=recv_sems.at[k],
                device_id=device(*DIRS[k]),
                device_id_type=MESH,
            )
            for k in order
        ]
        to = [exists(*DIRS[k]) for k in order]
        of = [exists(-DIRS[k][0], -DIRS[k][1]) for k in order]
        return list(zip(sent, to)), list(zip(sent, of))

    def combine(value, recv):
        def face(side):
            near = recv(SLOT[(side, 0)])[0:8, :]
            return near + edges(
                row_of(recv(SLOT[(side, 1)]), 7), row_of(recv(SLOT[(side, -1)]), 0)
            )

        out = []
        for i in range(8):
            term = value[i] + edges(
                row_of(recv(SLOT[(0, 1)]), i), row_of(recv(SLOT[(0, -1)]), i)
            )
            if i == 0:
                term += face(1)
            if i == 7:
                term += face(-1)
            out.append(term)
        return out

    def stage_drops():
        for b in range(REACH):
            for c in range(3):
                dsend[b, c : c + 1, :] = coord[3 * b + c]
                dsend[b, 3 + c : 4 + c, :] = dvel[3 * b + c]
            dsend[b, 6:7, :] = dprop[b, 0:1, :] * dprop[b, 1:2, :]
            dsend[b, 7:8, :] = jnp.where(
                lane[0:1] < cnt[0, 0, b], (elem[b] % EZ).astype(F32), -1.0
            )

    def block_copies(send, recv, send_sems, recv_sems, way):
        sent = [
            pltpu.make_async_remote_copy(
                src_ref=send.at[b],
                dst_ref=recv.at[b],
                send_sem=send_sems.at[b],
                recv_sem=recv_sems.at[b],
                device_id=device(way * (b - DRIFT), 0),
                device_id_type=MESH,
            )
            for b in AWAY
        ]
        to = [exists(way * (b - DRIFT), 0) for b in AWAY]
        of = [exists(-way * (b - DRIFT), 0) for b in AWAY]
        return list(zip(sent, to)), list(zip(sent, of))

    for load in loads[3:8]:
        load.wait()
    stage_drops()

    pl.semaphore_wait(barrier, greeted)
    first_out, first_in = copies(hsend, hrecv, s0, r0, ORDER)
    each(first_out, start)
    drops_out, drops_in = block_copies(dsend, drecv, sd, rd, 1)
    each(drops_out, start)

    khigh, klow = halves(
        jnp.concatenate([jnp.where(elane == e, tab[T_KT], 0.0) for e in range(EZ)], axis=0)
    )
    kz[0:128, 0:128] = khigh
    kz[0:128, 128:256] = klow
    kz[128:256, 0:128] = khigh
    kz[128:256, 128:256] = jnp.zeros((128, 128), BF16)

    def along_z(u):
        high, low = halves(jnp.concatenate(u, axis=0))
        both = jnp.dot(
            jnp.concatenate([high, low], axis=1), kz[...], preferred_element_type=F32
        )
        both = both[:, 0:128] + both[:, 128:256]
        return [both[8 * i : 8 * i + 8, :] for i in range(8)]

    def basis_block(b):
        def basis(r):
            value = tab[T_LAG]
            for m in range(8):
                value = value * jnp.where(sub == m, 1.0, r - float(NODES[m]))
            return value, turned(value, tab, T_DT)

        tile = drecv.at[b] if b != DRIFT else dsend.at[b]
        eid = row_of(tile, 7)
        lx[b], dx[b] = basis(row_of(tile, 0))
        ly[b], dy[b] = basis(row_of(tile, 1))
        span = slice(b * CAP, b * CAP + CAP)
        for part, ref in zip(basis(row_of(tile, 2)), (lz, ld)):
            high = part.astype(BF16).astype(F32)
            for piece, first in ((high, 0), (part - high, 128)):
                spread = jnp.concatenate(
                    [jnp.where(eid == float(e), piece, 0.0) for e in range(EZ)], axis=0
                )
                ref[first : first + 128, span] = spread.astype(BF16)

    def contract(planes, first, second):
        inner = total(row_of(first, i) * planes[i] for i in range(8))
        return jnp.sum(second[...] * inner, axis=0, keepdims=True)

    def stacked(value):
        high, low = halves(value)
        return jnp.concatenate(
            [
                jnp.concatenate([high, high], axis=1),
                jnp.concatenate([low, jnp.zeros_like(low)], axis=1),
            ],
            axis=0,
        )

    def base_values():
        loads[8].wait()
        left = stacked(jnp.concatenate([bvel[c, i] for c in range(3) for i in range(8)], axis=0))
        for b in range(REACH):
            span = slice(b * CAP, b * CAP + CAP)
            both = jnp.dot(left, lz[:, span], preferred_element_type=F32)
            both = both[0:192, :] + both[192:384, :]
            for c in range(3):
                planes = [both[64 * c + 8 * i : 64 * c + 8 * i + 8, :] for i in range(8)]
                fbase[b, c : c + 1, :] = contract(planes, lx.at[b], ly.at[b])

    basis_block(DRIFT)

    each(first_in, wait_recv)
    residual = combine(rhs, lambda k: hrecv.at[k])
    factor = {(0, 0): amet}
    for d in DIRS:
        factor[(-d[0], -d[1])] = row_of(hrecv.at[SLOT[d]], 8)
    own_x = amet + edges(factor[(0, -1)], factor[(0, 1)])
    side_x = {
        side: factor[(side, 0)] + edges(factor[(side, -1)], factor[(side, 1)])
        for side in (-1, 1)
    }
    side_y = edges(factor[(0, -1)], factor[(0, 1)])
    a_sum = [own_x + side_x[-1]] + [own_x] * 6 + [own_x + side_x[1]]
    a_y = [amet + factor[(-1, 0)]] + [amet] * 6 + [amet + factor[(1, 0)]]
    b_y = (
        [side_y + edges(factor[(-1, -1)], factor[(-1, 1)])]
        + [side_y] * 6
        + [side_y + edges(factor[(1, -1)], factor[(1, 1)])]
    )

    def present(ds, dc):
        return exists(ds, dc).astype(F32)

    count_y = 1.0 + edges(present(0, -1), present(0, 1))
    count_x = [1.0 + present(-1, 0)] + [1.0] * 6 + [1.0 + present(1, 0)]

    center = (UPPER_BOUND + LOWER_BOUND) / 2.0
    half_width = (UPPER_BOUND - LOWER_BOUND) / 2.0
    bound = center / half_width
    rho = 1.0 / bound

    wkj = wk * wj
    mass = [wkj * (count_x[i] * count_y) for i in range(8)]
    planes = {}
    for i in (0, 1, 7):
        planes[i] = (sum_z(wk * a_sum[i]), sum_z(tab[T_QK] * a_sum[i] + wk * (count_x[i] * count_y)))
    inv_diag, update = [], []
    for i in range(8):
        w_i, q_i = float(WEIGHTS[i]), float(QDIAG[i])
        first, second = planes[i if i in planes else 1]
        residual[i] = (w_i * wj) * residual[i]
        diagonal = (q_i * wj + w_i * tab[T_QJ]) * first + (w_i * wj) * second
        inv_diag.append(1.0 / diagonal)
        update.append(inv_diag[i] * residual[i] * (1.0 / center))
    iterate = update

    flights = []
    for sweep in range(SWEEPS):
        send, recv = nsend.at[sweep], nrecv.at[sweep]
        for i in range(8):
            ub[8 * i : 8 * i + 8, :] = update[i]
        lines = [ub[pl.ds(j, 8, stride=8), :] for j in range(8)]
        for k, (group, row) in enumerate([(update, 7), (update, 0), (lines, 7), (lines, 0)]):
            send[k] = total(float(STIFF[row, m]) * group[m] for m in range(8))
        out, into = copies(send, recv, s1.at[sweep], r1.at[sweep], [0, 1, 2, 3])
        each(out, start)
        flights.append(out)

        own = []
        flat, across = along_z(update), stiff_x(update)
        for i in range(8):
            w_i = float(WEIGHTS[i])
            own.append(
                wkj * own_x * across[i]
                + (w_i * wk) * a_y[i] * turned(update[i], tab, T_CY)
                + (w_i * wj) * a_sum[i] * flat[i]
                + w_i * mass[i] * update[i]
            )
        if sweep == 0:
            each(drops_in, wait_recv)
            basis_block(1)
            basis_block(3)
        elif sweep == 1:
            basis_block(0)
            basis_block(4)
        elif sweep == 2:
            base_values()

        each(into, wait_recv)
        for i in range(8):
            w_i = float(WEIGHTS[i])
            beside = edges(row_of(recv.at[2], i), row_of(recv.at[3], i))
            own[i] += (w_i * wk) * b_y[i] * beside
        own[0] += wkj * side_x[-1] * recv[0]
        own[7] += wkj * side_x[1] * recv[1]
        rho_next = 1.0 / (2.0 * bound - rho)
        for i in range(8):
            residual[i] = residual[i] - sum_z(own[i])
        update = [
            (rho_next * rho) * update[i]
            + (2.0 * rho_next / half_width) * (inv_diag[i] * residual[i])
            for i in range(8)
        ]
        rho = rho_next
        iterate = [iterate[i] + update[i] for i in range(8)]

    for i in range(8):
        p_out[i] = iterate[i]

    left = stacked(jnp.concatenate([amet * iterate[i] for i in range(8)], axis=0))
    forces = []
    for b in range(REACH):
        span = slice(b * CAP, b * CAP + CAP)

        def planes_of(ref):
            both = jnp.dot(left, ref[:, span], preferred_element_type=F32)
            both = both[0:64, :] + both[64:128, :]
            return [both[8 * i : 8 * i + 8, :] for i in range(8)]

        flat, slope = planes_of(lz), planes_of(ld)
        grads = [
            contract(flat, dx.at[b], ly.at[b]),
            contract(flat, lx.at[b], dy.at[b]),
            contract(slope, lx.at[b], ly.at[b]),
        ]
        tile = drecv.at[b] if b != DRIFT else dsend.at[b]
        force = []
        for c in range(3):
            fluid = fbase[b, c : c + 1, :] - grads[c]
            rsend[b, c : c + 1, :] = fluid
            force.append(tile[6:7, :] * (tile[3 + c : 4 + c, :] - fluid))
        forces.append(force)
    backs_out, backs_in = block_copies(rsend, rrecv, sr, rr, -1)
    each(backs_out, start)

    columns_high, columns_low = [], []
    for b in range(REACH):
        rows_ = []
        for c in range(3):
            weighted = wide(forces[b][c]) * ly[b]
            rows_ += [weighted * row_of(lx.at[b], i) for i in range(8)]
        high, low = halves(jnp.concatenate(rows_, axis=0))
        columns_high.append(high)
        columns_low.append(low)
    left = jnp.concatenate(
        [jnp.concatenate(columns_high, axis=1), jnp.concatenate(columns_low, axis=1)], axis=0
    )
    both = lax.dot_general(
        left, lz[...], (((1,), (1,)), ((), ())), preferred_element_type=F32
    )
    drag = both[0:192, 0:128] + both[0:192, 128:256] + both[192:384, 0:128]
    drag = [sum_z(drag[8 * i : 8 * i + 8, :]) for i in range(24)]
    for i in range(24):
        mb[8 * i : 8 * i + 8, :] = drag[i]
    for c in range(3):
        fsend[0, c] = drag[8 * c + 7]
        fsend[1, c] = drag[8 * c]
        fsend[2, c] = mb[pl.ds(64 * c + 7, 8, stride=8), :]
        fsend[3, c] = mb[pl.ds(64 * c, 8, stride=8), :]
    last_out, last_in = copies(fsend, frecv, s4, r4, ORDER)
    each(last_out, start)

    each(backs_in, wait_recv)
    for b in range(REACH):
        tile = rrecv.at[b] if b != DRIFT else rsend.at[b]
        for c in range(3):
            accel = dprop[b, 0:1, :] * (tile[c : c + 1, :] - dvel[3 * b + c])
            acc_out[3 * b + c] = jnp.where(lane[0:1] < cnt[0, 0, b], accel, 0.0)

    each(last_in, wait_recv)
    for c in range(3):
        value = combine(drag[8 * c : 8 * c + 8], lambda k: frecv.at[k, c])
        for i in range(8):
            m_out[c, i] = value[i]

    for sent in [first_out, drops_out] + flights + [backs_out, last_out]:
        each(sent, wait_send)


def deliver(p_in, m_in, acc_in, p_out, m_out, acc_out, sems):
    copies = [
        pltpu.make_async_copy(near, far, sems.at[n])
        for n, (near, far) in enumerate([(m_in, m_out), (p_in, p_out), (acc_in, acc_out)])
    ]
    for copy in copies:
        copy.start()
    for copy in copies:
        copy.wait()


def on_device(source, metric, base, elem, coord, dvel, dprop, counts):
    vmem = pl.BlockSpec(memory_space=pltpu.VMEM)
    hbm = pl.BlockSpec(memory_space=pltpu.HBM)
    dma = pltpu.SemaphoreType.DMA
    elem = elem.reshape(REACH, 1, CAP)
    coord = coord.reshape(REACH * 3, 1, CAP)
    dvel = dvel.reshape(REACH * 3, 1, CAP)
    dprop = dprop.reshape(REACH, 2, CAP)
    tile = (8, 128)
    blocks = pltpu.VMEM((REACH,) + tile, F32)
    shapes = (
        jax.ShapeDtypeStruct((8, 8, 128), F32),
        jax.ShapeDtypeStruct((3, 8, 8, 128), F32),
        jax.ShapeDtypeStruct((REACH * 3, 1, CAP), F32),
    )
    operands = (source, metric, base, elem, coord, dvel, dprop, counts)
    operands += (jnp.asarray(constant_tiles()),)
    outs = pl.pallas_call(
        kernel,
        out_shape=shapes,
        in_specs=[hbm] * 9,
        out_specs=(vmem,) * 3,
        scratch_shapes=[
            pltpu.VMEM((8, 8, 128), F32),
            pltpu.SMEM((1, 1, EZ), F32),
            pltpu.VMEM((3, 8, 8, 128), F32),
            pltpu.VMEM((REACH, 1, CAP), jnp.int32),
            pltpu.VMEM((REACH * 3, 1, CAP), F32),
            pltpu.VMEM((REACH * 3, 1, CAP), F32),
            pltpu.VMEM((REACH, 2, CAP), F32),
            pltpu.SMEM((1, 1, REACH), jnp.int32),
            pltpu.VMEM((PACKED,) + tile, F32),
            pltpu.VMEM((TILES,) + tile, F32),
            pltpu.VMEM((64, 128), F32),
            pltpu.VMEM((192, 128), F32),
            pltpu.VMEM((256, 256), BF16),
            pltpu.VMEM((256, REACH * CAP), BF16),
            pltpu.VMEM((256, REACH * CAP), BF16),
            blocks,
            blocks,
            blocks,
            blocks,
            blocks,
            pltpu.VMEM((4, 16, 128), F32),
            pltpu.VMEM((8, 16, 128), F32),
            pltpu.VMEM((SWEEPS, 4) + tile, F32),
            pltpu.VMEM((SWEEPS, 4) + tile, F32),
            pltpu.VMEM((4, 3) + tile, F32),
            pltpu.VMEM((8, 3) + tile, F32),
            blocks,
            blocks,
            blocks,
            blocks,
            dma((9,)),
            dma((8,)),
            dma((8,)),
            dma((SWEEPS, 4)),
            dma((SWEEPS, 4)),
            dma((8,)),
            dma((8,)),
            dma((REACH,)),
            dma((REACH,)),
            dma((REACH,)),
            dma((REACH,)),
        ],
        compiler_params=pltpu.CompilerParams(
            collective_id=0, has_side_effects=True, vmem_limit_bytes=32 * 1024 * 1024
        ),
    )(*[pltpu.with_memory_space_constraint(operand, pltpu.HBM) for operand in operands])
    pressure, momentum, accel = pl.pallas_call(
        deliver,
        out_shape=shapes,
        in_specs=[vmem] * 3,
        out_specs=(hbm,) * 3,
        scratch_shapes=[dma((3,))],
        compiler_params=pltpu.CompilerParams(vmem_limit_bytes=1024 * 1024),
    )(*outs)
    return pressure, momentum, accel.reshape(1, 1, REACH, 3, CAP)


def solution(mesh):
    in_specs = (
        P("stream", "cross", None),
        P("stream", "cross", None),
        P(None, "stream", "cross", None),
        P("stream", "cross", None, None),
        P("stream", "cross", None, None, None),
        P("stream", "cross", None, None, None),
        P("stream", "cross", None, None, None),
        P("stream", "cross", None),
    )
    out_specs = (
        P("stream", "cross", None),
        P(None, "stream", "cross", None),
        P("stream", "cross", None, None, None),
    )
    return jax.shard_map(
        on_device, mesh=mesh, in_specs=in_specs, out_specs=out_specs, check_vma=False
    )
```

time: 46.9 us -> 33.6 us (0.72)
  the two profiles are of different devices: /device:TPU:1 before, /device:TPU:7 now
where the time goes in v1:
time: 33.6 us; the launch traced here: 33.4 us
  Pallas kernels  32.8 us (98%)
  between operations  0.64 us (2%)
    pallas_call x1, Pallas kernels, on_device(): pl.pallas_call(kernel, out_shape=shapes, in_specs=[hbm] * 9, out_specs=(v...  32.1 us
    pallas_call x1, Pallas kernels, on_device(): pl.pallas_call(deliver, out_shape=shapes, in_specs=[vmem] * 3, out_specs=...  0.68 us

profile of v1, /device:TPU:7, one launch (start us, length us, event | category | flops | bytes accessed | tf_op | source)
XLA Modules:
  0.0 33.4 jit_solution(10758750715427115888)
XLA Ops:
  0.6 32.1 %shard_map.112 = (f32[8,8,128]{2,1,0:T(8,128)S(1)}, f32[3,8,8,128]{3,2,1,0:T(8,128)S(1)}, f32[15,1,128]{2,1,0:T(1,128)S(1)}) custom-call(f32[8,8,128]{2,1,0:T(8,128)} %src_h.1, f32[1,1,16]{2,1,0:T(1,128)} %met_h.1, f32[3,8,8,128]{3,2,1,0:T(8,128)} %bvel_h.1, s32[5,1,128]{2,1,0:T(1,128)} %bitcast.10, f32[15,1,128]{2,1,0:T(1,128)} %bitcast.7, ...), custom_call_target="tpu_custom_call" | custom-call | tf_op jit(solution)/shard_map/pallas_call | solution.py:567
  32.8 0.7 %shard_map.113 = (f32[8,8,128]{2,1,0:T(8,128)}, f32[3,8,8,128]{3,2,1,0:T(8,128)}, f32[15,1,128]{2,1,0:T(1,128)}) custom-call(f32[8,8,128]{2,1,0:T(8,128)S(1)} %get-tuple-element.9.p_in, f32[3,8,8,128]{3,2,1,0:T(8,128)S(1)} %get-tuple-element.10.m_in, f32[15,1,128]{2,1,0:T(1,128)S(1)} %get-tuple-element.11.acc_in), custom_call_target="tpu_custom_call" | custom-call | tf_op jit(solution)/shard_map/pallas_call | solution.py:619

commit v2 on v1

--- a/solution.py
+++ b/solution.py
@@ -32,6 +32,11 @@
 DIRS = [(1, 0), (-1, 0), (0, 1), (0, -1), (1, 1), (1, -1), (-1, 1), (-1, -1)]
 SLOT = {d: k for k, d in enumerate(DIRS)}
 ORDER = [4, 5, 6, 7, 0, 1, 2, 3]
+FACES = DIRS[:4]
+CORNERS = DIRS[4:]
+PLACE = {(1, 0): 0, (0, 1): 1, (-1, 0): 2, (0, -1): 3}
+PAIR = {(1, 1): 0, (-1, 1): 1, (-1, -1): 2, (1, -1): 3}
+COEF = {(-1, 0): 0, (1, 0): 2, (0, -1): 4, (0, 1): 6}
 AWAY = [0, 4, 1, 3]
 
 
@@ -64,8 +69,8 @@
 QDIAG = np.diag(STIFF)
 
 PACKED = 5
-T_WK, T_QK, T_KT, T_ZM, T_WJ, T_QJ, T_CY, T_DT, T_LAG = 0, 1, 2, 3, 4, 5, 6, 14, 22
-TILES = 23
+T_WK, T_QK, T_KT, T_ZM, T_WJ, T_QJ, T_CY, T_DT, T_LAG, T_END = 0, 1, 2, 3, 4, 5, 6, 14, 22, 23
+TILES = 25
 
 
 def constant_tiles():
@@ -86,6 +91,8 @@
         columns[:, T_DT + turn] = DERIV[(row - turn) % 8, row]
     gaps = NODES[:, None] - NODES[None, :] + np.eye(8)
     columns[:, T_LAG] = 1.0 / gaps.prod(1)
+    columns[0:7, T_END] = STIFF[7, 0:7]
+    columns[1:8, T_END + 1] = STIFF[0, 1:8]
     return tiles.astype(np.float32)
 
 
@@ -137,7 +144,8 @@
     src, met, bvel, elem, coord, dvel, dprop, cnt, pack, tab,
     ub, mb, kz, lz, ld, lx, dx, ly, dy, fbase,
     hsend, hrecv, nsend, nrecv, fsend, frecv, dsend, drecv, rsend, rrecv,
-    si, s0, r0, s1, r1, s4, r4, sd, rd, sr, rr,
+    csend, crecv, tsend, trecv, farrecv, crnrecv,
+    si, s0, r0, s1, r1, s4, r4, sd, rd, sr, rr, sc, rc, st, rt, sf, rf, sk, rk,
 ):
     slabs, cols = lax.axis_size("stream"), lax.axis_size("cross")
     slab, col = lax.axis_index("stream"), lax.axis_index("cross")
@@ -174,15 +182,15 @@
     def wait_send(copy):
         copy.wait_send()
 
-    inside = (slab >= DRIFT) & (slab < slabs - DRIFT) & (col > 0) & (col < cols - 1)
+    inside = (slab >= 2) & (slab < slabs - 2) & (col >= 2) & (col < cols - 2)
 
     @pl.when(jnp.logical_not(inside))
     def _():
-        for ref in (hrecv, nrecv, frecv, drecv, rrecv):
+        for ref in (hrecv, nrecv, frecv, drecv, rrecv, crecv, trecv, farrecv, crnrecv):
             ref[...] = jnp.zeros_like(ref)
 
     barrier = pltpu.get_barrier_semaphore()
-    partners = DIRS + [(2, 0), (-2, 0)]
+    partners = DIRS + [(2, 0), (-2, 0), (0, 2), (0, -2)]
     greeted = jnp.int32(0)
     for d in partners:
         there = exists(*d)
@@ -374,18 +382,14 @@
     for d in DIRS:
         factor[(-d[0], -d[1])] = row_of(hrecv.at[SLOT[d]], 8)
     own_x = amet + edges(factor[(0, -1)], factor[(0, 1)])
-    side_x = {
-        side: factor[(side, 0)] + edges(factor[(side, -1)], factor[(side, 1)])
-        for side in (-1, 1)
+    a_y = [amet + factor[(-1, 0)]] + [amet] * 6 + [amet + factor[(1, 0)]]
+    side = {
+        (t, 0): factor[(t, 0)] + edges(factor[(t, -1)], factor[(t, 1)]) for t in (-1, 1)
     }
-    side_y = edges(factor[(0, -1)], factor[(0, 1)])
-    a_sum = [own_x + side_x[-1]] + [own_x] * 6 + [own_x + side_x[1]]
-    a_y = [amet + factor[(-1, 0)]] + [amet] * 6 + [amet + factor[(1, 0)]]
-    b_y = (
-        [side_y + edges(factor[(-1, -1)], factor[(-1, 1)])]
-        + [side_y] * 6
-        + [side_y + edges(factor[(1, -1)], factor[(1, 1)])]
-    )
+    side |= {
+        (0, t): factor[(0, t)] + edges(factor[(-1, t)], factor[(1, t)]) for t in (-1, 1)
+    }
+    a_sum = [own_x + side[(-1, 0)]] + [own_x] * 6 + [own_x + side[(1, 0)]]
 
     def present(ds, dc):
         return exists(ds, dc).astype(F32)
@@ -413,55 +417,173 @@
         update.append(inv_diag[i] * residual[i] * (1.0 / center))
     iterate = update
 
-    flights = []
-    for sweep in range(SWEEPS):
-        send, recv = nsend.at[sweep], nrecv.at[sweep]
+    across = {d: wkj * side[d] for d in FACES}
+    for i in range(8):
+        mb[8 * i : 8 * i + 8, :] = inv_diag[i]
+    inv_face = {
+        (-1, 0): inv_diag[0],
+        (1, 0): inv_diag[7],
+        (0, -1): mb[pl.ds(0, 8, stride=8), :],
+        (0, 1): mb[pl.ds(7, 8, stride=8), :],
+    }
+    for d in FACES:
+        csend[COEF[d]] = across[d]
+        csend[COEF[d] + 1] = inv_face[d]
+
+    def to_faces(source, recv, send_sems, recv_sems, dirs):
+        sent = [
+            pltpu.make_async_remote_copy(
+                src_ref=source(d),
+                dst_ref=recv.at[n],
+                send_sem=send_sems.at[n],
+                recv_sem=recv_sems.at[n],
+                device_id=device(*d),
+                device_id_type=MESH,
+            )
+            for n, d in enumerate(dirs)
+        ]
+        to = [exists(*d) for d in dirs]
+        of = [exists(-d[0], -d[1]) for d in dirs]
+        return list(zip(sent, to)), list(zip(sent, of))
+
+    def lines_of(u):
         for i in range(8):
-            ub[8 * i : 8 * i + 8, :] = update[i]
-        lines = [ub[pl.ds(j, 8, stride=8), :] for j in range(8)]
-        for k, (group, row) in enumerate([(update, 7), (update, 0), (lines, 7), (lines, 0)]):
-            send[k] = total(float(STIFF[row, m]) * group[m] for m in range(8))
-        out, into = copies(send, recv, s1.at[sweep], r1.at[sweep], [0, 1, 2, 3])
-        each(out, start)
-        flights.append(out)
-
-        own = []
-        flat, across = along_z(update), stiff_x(update)
+            ub[8 * i : 8 * i + 8, :] = u[i]
+        return [ub[pl.ds(j, 8, stride=8), :] for j in range(8)]
+
+    def ends(u, send, inner):
+        lines = lines_of(u)
+        for d, group, row in (
+            ((1, 0), u, 7), ((-1, 0), u, 0), ((0, 1), lines, 7), ((0, -1), lines, 0)
+        ):
+            send[PLACE[d]] = total(
+                float(STIFF[row, m]) * group[m] for m in range(8) if not (inner and m == row)
+            )
+
+    def own_part(u):
+        flat, slope = along_z(u), stiff_x(u)
+        out = []
         for i in range(8):
             w_i = float(WEIGHTS[i])
-            own.append(
-                wkj * own_x * across[i]
-                + (w_i * wk) * a_y[i] * turned(update[i], tab, T_CY)
-                + (w_i * wj) * a_sum[i] * flat[i]
-                + w_i * mass[i] * update[i]
+            out.append(
+                sum_z(
+                    wkj * own_x * slope[i]
+                    + (w_i * wk) * a_y[i] * turned(u[i], tab, T_CY)
+                    + (w_i * wj) * a_sum[i] * flat[i]
+                    + w_i * mass[i] * u[i]
+                )
             )
-        if sweep == 0:
-            each(drops_in, wait_recv)
-            basis_block(1)
-            basis_block(3)
-        elif sweep == 1:
-            basis_block(0)
-            basis_block(4)
-        elif sweep == 2:
-            base_values()
-
-        each(into, wait_recv)
-        for i in range(8):
-            w_i = float(WEIGHTS[i])
-            beside = edges(row_of(recv.at[2], i), row_of(recv.at[3], i))
-            own[i] += (w_i * wk) * b_y[i] * beside
-        own[0] += wkj * side_x[-1] * recv[0]
-        own[7] += wkj * side_x[1] * recv[1]
-        rho_next = 1.0 / (2.0 * bound - rho)
-        for i in range(8):
-            residual[i] = residual[i] - sum_z(own[i])
-        update = [
-            (rho_next * rho) * update[i]
-            + (2.0 * rho_next / half_width) * (inv_diag[i] * residual[i])
+        return out
+
+    def less_beside(value, flow):
+        part = {d: sum_z(across[d] * flow[d]) for d in FACES}
+        out = [
+            value[i]
+            - edges(wide(part[(0, -1)][i : i + 1, :]), wide(part[(0, 1)][i : i + 1, :]))
             for i in range(8)
         ]
+        out[0] -= part[(-1, 0)]
+        out[7] -= part[(1, 0)]
+        return out
+
+    steps = []
+    for sweep in range(SWEEPS):
+        rho_next = 1.0 / (2.0 * bound - rho)
+        steps.append((rho_next * rho, 2.0 * rho_next / half_width))
         rho = rho_next
-        iterate = [iterate[i] + update[i] for i in range(8)]
+
+    def advanced(u, left, step):
+        return [step[0] * u[i] + step[1] * (inv_diag[i] * left[i]) for i in range(8)]
+
+    def opposite(d):
+        return (-d[0], -d[1])
+
+    ends(update, nsend.at[0], False)
+    near_out, near_in = to_faces(
+        lambda d: nsend.at[0, PLACE[d]], nrecv.at[0], s1.at[0], r1.at[0], FACES
+    )
+    each(near_out, start)
+    coef_out, coef_in = to_faces(lambda d: csend, crecv, sc, rc, FACES)
+    each(coef_out, start)
+    own = own_part(update)
+    residual = [residual[i] - own[i] for i in range(8)]
+    each(drops_in, wait_recv)
+    basis_block(1)
+    basis_block(3)
+    each(near_in, wait_recv)
+    residual = less_beside(residual, {opposite(d): nrecv[0, n] for n, d in enumerate(FACES)})
+    update = advanced(update, residual, steps[0])
+    iterate = [iterate[i] + update[i] for i in range(8)]
+    flights = [near_out, coef_out]
+
+    send = nsend.at[1]
+    ends(update, send, False)
+    send[4] = send[0]
+    far_out, far_in = to_faces(
+        lambda d: send.at[PLACE[(d[0] // 2, d[1] // 2)]],
+        farrecv, sf, rf, [(2 * x, 2 * y) for x, y in FACES],
+    )
+    corner_out, corner_in = to_faces(
+        lambda d: send.at[pl.ds(PAIR[d], 2)], crnrecv, sk, rk, CORNERS
+    )
+    near_out, near_in = to_faces(lambda d: send.at[PLACE[d]], nrecv.at[1], s1.at[1], r1.at[1], FACES)
+    each(far_out, start)
+    each(corner_out, start)
+    each(near_out, start)
+    own = own_part(update)
+    residual = [residual[i] - own[i] for i in range(8)]
+    ends(advanced(update, residual, steps[1]), tsend, True)
+    tilde_out, tilde_in = to_faces(lambda d: tsend.at[PLACE[d]], trecv, st, rt, FACES)
+    each(tilde_out, start)
+    flights += [far_out, corner_out, near_out, tilde_out]
+    basis_block(0)
+    basis_block(4)
+    base_values()
+
+    each(near_in, wait_recv)
+    residual = less_beside(residual, {opposite(d): nrecv[1, n] for n, d in enumerate(FACES)})
+    update = advanced(update, residual, steps[1])
+    iterate = [iterate[i] + update[i] for i in range(8)]
+    lines = lines_of(update)
+    own = own_part(update)
+    residual = [residual[i] - own[i] for i in range(8)]
+
+    for arrived in (coef_in, far_in, corner_in, tilde_in):
+        each(arrived, wait_recv)
+
+    def from_corner(at, along):
+        d = opposite(at)
+        return crnrecv[CORNERS.index(d), (PLACE[along] - PAIR[d]) % 4]
+
+    flow = {}
+    for n, d in enumerate(FACES):
+        at = opposite(d)
+        coef = crecv.at[n]
+
+        def change(face, across_it):
+            spread = sum_z(coef[COEF[face]] * across_it)
+            return (-steps[1][1]) * (coef[COEF[face] + 1] * spread)
+
+        forward = d[0] + d[1] > 0
+        far_weight = float(STIFF[7, 0] if forward else STIFF[0, 7])
+        near_weight = float(STIFF[7, 7] if forward else STIFF[0, 0])
+        weights = tab[T_END if forward else T_END + 1]
+        rims = []
+        for t in (-1, 1):
+            rim = (0, t) if d[0] else (t, 0)
+            corner = (at[0] + rim[0], at[1] + rim[1])
+            changed = change(rim, from_corner(corner, opposite(rim)))
+            rims.append(wide(jnp.sum(weights * changed, axis=0, keepdims=True)))
+        if d[0]:
+            shared = update[0 if forward else 7]
+        else:
+            shared = lines[0 if forward else 7]
+        flow[at] = (
+            trecv[n] + far_weight * change(at, farrecv[n]) + edges(*rims) + near_weight * shared
+        )
+    residual = less_beside(residual, flow)
+    update = advanced(update, residual, steps[2])
+    iterate = [iterate[i] + update[i] for i in range(8)]
 
     for i in range(8):
         p_out[i] = iterate[i]
@@ -592,25 +714,39 @@
             blocks,
             pltpu.VMEM((4, 16, 128), F32),
             pltpu.VMEM((8, 16, 128), F32),
-            pltpu.VMEM((SWEEPS, 4) + tile, F32),
-            pltpu.VMEM((SWEEPS, 4) + tile, F32),
+            pltpu.VMEM((2, 5) + tile, F32),
+            pltpu.VMEM((2, 4) + tile, F32),
             pltpu.VMEM((4, 3) + tile, F32),
             pltpu.VMEM((8, 3) + tile, F32),
             blocks,
             blocks,
             blocks,
             blocks,
+            pltpu.VMEM((8,) + tile, F32),
+            pltpu.VMEM((4, 8) + tile, F32),
+            pltpu.VMEM((4,) + tile, F32),
+            pltpu.VMEM((4,) + tile, F32),
+            pltpu.VMEM((4,) + tile, F32),
+            pltpu.VMEM((4, 2) + tile, F32),
             dma((9,)),
             dma((8,)),
             dma((8,)),
-            dma((SWEEPS, 4)),
-            dma((SWEEPS, 4)),
+            dma((2, 4)),
+            dma((2, 4)),
             dma((8,)),
             dma((8,)),
             dma((REACH,)),
             dma((REACH,)),
             dma((REACH,)),
             dma((REACH,)),
+            dma((4,)),
+            dma((4,)),
+            dma((4,)),
+            dma((4,)),
+            dma((4,)),
+            dma((4,)),
+            dma((4,)),
+            dma((4,)),
         ],
         compiler_params=pltpu.CompilerParams(
             collective_id=0, has_side_effects=True, vmem_limit_bytes=32 * 1024 * 1024

time: 33.6 us -> 31.8 us (0.946)
  Pallas kernels: 32.8 us -> 31 us
    pallas_call x1, Pallas kernels: 32.1 us -> 30.3 us  [on_device(): pl.pallas_call(kernel, out_shape=shapes, in_specs=[hbm] * 9, out_specs=(v...]
where the time goes in v2:
time: 31.8 us; the launch traced here: 31.6 us
  Pallas kernels  31 us (97%)
  between operations  0.64 us (2%)
    pallas_call x1, Pallas kernels, on_device(): pl.pallas_call(kernel, out_shape=shapes, in_specs=[hbm] * 9, out_specs=(v...  30.3 us
    pallas_call x1, Pallas kernels, on_device(): pl.pallas_call(deliver, out_shape=shapes, in_specs=[vmem] * 3, out_specs=...  0.68 us

profile of v2, /device:TPU:7, one launch (start us, length us, event | category | flops | bytes accessed | tf_op | source)
XLA Modules:
  0.0 31.6 jit_solution(16049508176852785323)
XLA Ops:
  0.6 30.3 %shard_map.112 = (f32[8,8,128]{2,1,0:T(8,128)S(1)}, f32[3,8,8,128]{3,2,1,0:T(8,128)S(1)}, f32[15,1,128]{2,1,0:T(1,128)S(1)}) custom-call(f32[8,8,128]{2,1,0:T(8,128)} %src_h.1, f32[1,1,16]{2,1,0:T(1,128)} %met_h.1, f32[3,8,8,128]{3,2,1,0:T(8,128)} %bvel_h.1, s32[5,1,128]{2,1,0:T(1,128)} %bitcast.10, f32[15,1,128]{2,1,0:T(1,128)} %bitcast.7, ...), custom_call_target="tpu_custom_call" | custom-call | tf_op jit(solution)/shard_map/pallas_call | solution.py:689
  31.0 0.7 %shard_map.113 = (f32[8,8,128]{2,1,0:T(8,128)}, f32[3,8,8,128]{3,2,1,0:T(8,128)}, f32[15,1,128]{2,1,0:T(1,128)}) custom-call(f32[8,8,128]{2,1,0:T(8,128)S(1)} %get-tuple-element.9.p_in, f32[3,8,8,128]{3,2,1,0:T(8,128)S(1)} %get-tuple-element.10.m_in, f32[15,1,128]{2,1,0:T(1,128)S(1)} %get-tuple-element.11.acc_in), custom_call_target="tpu_custom_call" | custom-call | tf_op jit(solution)/shard_map/pallas_call | solution.py:755

commit v3 on v2

--- a/solution.py
+++ b/solution.py
@@ -1,5 +1,3 @@
-import functools
-
 import jax
 import jax.numpy as jnp
 import numpy as np
@@ -29,11 +27,9 @@
 BF16 = jnp.bfloat16
 MESH = pl.DeviceIdType.MESH
 
-DIRS = [(1, 0), (-1, 0), (0, 1), (0, -1), (1, 1), (1, -1), (-1, 1), (-1, -1)]
-SLOT = {d: k for k, d in enumerate(DIRS)}
-ORDER = [4, 5, 6, 7, 0, 1, 2, 3]
-FACES = DIRS[:4]
-CORNERS = DIRS[4:]
+FACES = [(1, 0), (-1, 0), (0, 1), (0, -1)]
+CORNERS = [(1, 1), (1, -1), (-1, 1), (-1, -1)]
+AWAY = [0, 4, 1, 3]
 PLACE = {(1, 0): 0, (0, 1): 1, (-1, 0): 2, (0, -1): 3}
 PAIR = {(1, 1): 0, (-1, 1): 1, (-1, -1): 2, (1, -1): 3}
 COEF = {(-1, 0): 0, (1, 0): 2, (0, -1): 4, (0, 1): 6}
@@ -143,21 +139,20 @@
     p_out, m_out, acc_out,
     src, met, bvel, elem, coord, dvel, dprop, cnt, pack, tab,
     ub, mb, kz, lz, ld, lx, dx, ly, dy, fbase,
-    hsend, hrecv, nsend, nrecv, fsend, frecv, dsend, drecv, rsend, rrecv,
-    csend, crecv, tsend, trecv, farrecv, crnrecv,
-    si, s0, r0, s1, r1, s4, r4, sd, rd, sr, rr, sc, rc, st, rt, sf, rf, sk, rk,
+    hsend, hrecv, hcs, hcr, nsend, nrecv, fsend, frecv, fcs, fcr,
+    dsend, drecv, rsend, rrecv, csend, crecv, tsend, trecv, grecv, zeros, zero_rows,
+    *rest,
 ):
+    *spare, ledger, load_ledger, si, send_sems, recv_sems = rest
     slabs, cols = lax.axis_size("stream"), lax.axis_size("cross")
     slab, col = lax.axis_index("stream"), lax.axis_index("cross")
 
     loads = [
         pltpu.make_async_copy(far, near, si.at[n])
-        for n, (far, near) in enumerate(
-            [
-                (tab_h, pack), (met_h, met), (src_h, src), (cnt_h, cnt), (elem_h, elem),
-                (coord_h, coord), (dvel_h, dvel), (dprop_h, dprop), (bvel_h, bvel),
-            ]
-        )
+        for far, near, n in [
+            (tab_h, pack, 0), (src_h, src, 1), (met_h, met, 2), (cnt_h, cnt, 3), (elem_h, elem, 4),
+            (coord_h, coord, 4), (dvel_h, dvel, 4), (dprop_h, dprop, 4), (bvel_h, bvel, 5),
+        ]
     ]
     for load in loads:
         load.start()
@@ -169,28 +164,45 @@
         found = (slab + ds >= 0) & (slab + ds < slabs)
         return found & (col + dc >= 0) & (col + dc < cols)
 
-    def each(copies, act):
-        for copy, there in copies:
-            pl.when(there)(functools.partial(act, copy))
-
-    def start(copy):
-        copy.start()
-
-    def wait_recv(copy):
-        copy.wait_recv()
-
-    def wait_send(copy):
-        copy.wait_send()
-
     inside = (slab >= 2) & (slab < slabs - 2) & (col >= 2) & (col < cols - 2)
-
-    @pl.when(jnp.logical_not(inside))
-    def _():
-        for ref in (hrecv, nrecv, frecv, drecv, rrecv, crecv, trecv, farrecv, crnrecv):
-            ref[...] = jnp.zeros_like(ref)
+    groups = []
+
+    class Group:
+        def __init__(self, recv, messages):
+            self.recv, self.messages = recv, messages
+            self.sem = recv_sems.at[len(groups)]
+            self.spare = spare[len(groups)]
+            groups.append(self)
+
+        def start(self):
+            for d, source, slot in self.messages:
+                copy = pltpu.make_async_remote_copy(
+                    src_ref=source,
+                    dst_ref=self.recv.at[slot],
+                    send_sem=send_sems.at[0],
+                    recv_sem=self.sem,
+                    device_id=device(*d),
+                    device_id_type=MESH,
+                )
+                pl.when(exists(*d))(copy.start)
+
+        def wait(self):
+            pltpu.make_async_copy(self.recv, self.recv, self.sem).wait()
+
+        def fill(self):
+            for d, _, slot in self.messages:
+                near, away = self.recv.at[slot], self.spare.at[slot]
+                pool = zero_rows if near.shape[-2] == 1 else zeros
+                none = pool.at[0] if len(near.shape) == 2 else pool.at[pl.ds(0, near.shape[0])]
+                pl.when(jnp.logical_not(exists(-d[0], -d[1])))(
+                    pltpu.make_async_copy(none, near, self.sem).start
+                )
+                pl.when(jnp.logical_not(exists(*d)))(
+                    pltpu.make_async_copy(none, away, send_sems.at[0]).start
+                )
 
     barrier = pltpu.get_barrier_semaphore()
-    partners = DIRS + [(2, 0), (-2, 0), (0, 2), (0, -2)]
+    partners = FACES + CORNERS + [(2, 0), (-2, 0), (0, 2), (0, -2)]
     greeted = jnp.int32(0)
     for d in partners:
         there = exists(*d)
@@ -223,53 +235,69 @@
     def row_of(ref, i):
         return wide(ref[i : i + 1, :])
 
-    loads[1].wait()
+    loads[2].wait()
     amet = jnp.zeros((8, 128), F32)
     for e in range(EZ):
         amet = jnp.where(elane == e, met[0, 0, e], amet)
-    loads[2].wait()
+    loads[1].wait()
     rhs = [sum_z(wk * src[i]) for i in range(8)]
 
-    for i in range(8):
-        ub[8 * i : 8 * i + 8, :] = rhs[i]
-    hsend[0, 0:8, :] = rhs[7]
-    hsend[1, 0:8, :] = rhs[0]
-    hsend[2, 0:8, :] = ub[pl.ds(7, 8, stride=8), :]
-    hsend[3, 0:8, :] = ub[pl.ds(0, 8, stride=8), :]
-    for k in range(4):
-        hsend[k, 8:16, :] = amet
-
-    def tile_of(d):
-        return SLOT[(d[0], 0)] if d[0] else SLOT[d]
-
-    def copies(send, recv, send_sems, recv_sems, order):
-        sent = [
-            pltpu.make_async_remote_copy(
-                src_ref=send.at[tile_of(DIRS[k])],
-                dst_ref=recv.at[k],
-                send_sem=send_sems.at[k],
-                recv_sem=recv_sems.at[k],
-                device_id=device(*DIRS[k]),
-                device_id_type=MESH,
+    def lines_of(u):
+        for i in range(8):
+            ub[8 * i : 8 * i + 8, :] = u[i]
+        return [ub[pl.ds(j, 8, stride=8), :] for j in range(8)]
+
+    def edge_row(d):
+        return 7 if d > 0 else 0
+
+    lines = lines_of(rhs)
+    for n, d in enumerate(FACES):
+        hsend[n, 0] = (rhs if d[0] else lines)[edge_row(d[0] + d[1])]
+        hsend[n, 1] = amet
+    for n, d in enumerate(CORNERS):
+        row = edge_row(d[1])
+        hcs[n, 0] = rhs[edge_row(d[0])][row : row + 1, :]
+        hcs[n, 1] = amet[0:1, :]
+
+    def slots(dirs, source):
+        return [(d, source(n, d), n) for n, d in enumerate(dirs)]
+
+    blocks_to = [((b - DRIFT, 0), dsend.at[b], n) for n, b in enumerate(AWAY)]
+    blocks_back = [((DRIFT - b, 0), rsend.at[b], n) for n, b in enumerate(AWAY)]
+    first, second = nsend.at[0], nsend.at[1]
+    heads = Group(hrecv, slots(FACES, lambda n, d: hsend.at[n]))
+    head_corners = Group(hcr, slots(CORNERS, lambda n, d: hcs.at[n]))
+    drops = Group(drecv, blocks_to)
+    near_one = Group(nrecv.at[0], slots(FACES, lambda n, d: first.at[PLACE[d]]))
+    coefs = Group(crecv, slots(FACES, lambda n, d: csend))
+    near_two = Group(nrecv.at[1], slots(FACES, lambda n, d: second.at[PLACE[d]]))
+    far_two = Group(
+        grecv,
+        [((2 * d[0], 2 * d[1]), second.at[PLACE[d]], n) for n, d in enumerate(FACES)]
+        + [(d, second.at[pl.ds(PAIR[d], 2)], pl.ds(4 + 2 * n, 2)) for n, d in enumerate(CORNERS)],
+    )
+    tilde = Group(trecv, slots(FACES, lambda n, d: tsend.at[PLACE[d]]))
+    backs = Group(rrecv, blocks_back)
+    tails = Group(frecv, slots(FACES, lambda n, d: fsend.at[n]))
+    tail_corners = Group(fcr, slots(CORNERS, lambda n, d: fcs.at[n]))
+
+    @pl.when(jnp.logical_not(inside))
+    def _():
+        zeros[...] = jnp.zeros_like(zeros)
+        zero_rows[...] = jnp.zeros_like(zero_rows)
+        for group in groups:
+            group.fill()
+
+    def combine(value, recv, corner):
+        def face(t):
+            return recv(FACES.index((t, 0))) + edges(
+                wide(corner(CORNERS.index((t, 1)))), wide(corner(CORNERS.index((t, -1))))
             )
-            for k in order
-        ]
-        to = [exists(*DIRS[k]) for k in order]
-        of = [exists(-DIRS[k][0], -DIRS[k][1]) for k in order]
-        return list(zip(sent, to)), list(zip(sent, of))
-
-    def combine(value, recv):
-        def face(side):
-            near = recv(SLOT[(side, 0)])[0:8, :]
-            return near + edges(
-                row_of(recv(SLOT[(side, 1)]), 7), row_of(recv(SLOT[(side, -1)]), 0)
-            )
-
+
+        low, high = recv(FACES.index((0, 1))), recv(FACES.index((0, -1)))
         out = []
         for i in range(8):
-            term = value[i] + edges(
-                row_of(recv(SLOT[(0, 1)]), i), row_of(recv(SLOT[(0, -1)]), i)
-            )
+            term = value[i] + edges(wide(low[i : i + 1, :]), wide(high[i : i + 1, :]))
             if i == 0:
                 term += face(1)
             if i == 7:
@@ -287,31 +315,14 @@
                 lane[0:1] < cnt[0, 0, b], (elem[b] % EZ).astype(F32), -1.0
             )
 
-    def block_copies(send, recv, send_sems, recv_sems, way):
-        sent = [
-            pltpu.make_async_remote_copy(
-                src_ref=send.at[b],
-                dst_ref=recv.at[b],
-                send_sem=send_sems.at[b],
-                recv_sem=recv_sems.at[b],
-                device_id=device(way * (b - DRIFT), 0),
-                device_id_type=MESH,
-            )
-            for b in AWAY
-        ]
-        to = [exists(way * (b - DRIFT), 0) for b in AWAY]
-        of = [exists(-way * (b - DRIFT), 0) for b in AWAY]
-        return list(zip(sent, to)), list(zip(sent, of))
-
-    for load in loads[3:8]:
-        load.wait()
+    loads[3].wait()
+    pltpu.make_async_copy(load_ledger, load_ledger, si.at[4]).wait()
     stage_drops()
 
     pl.semaphore_wait(barrier, greeted)
-    first_out, first_in = copies(hsend, hrecv, s0, r0, ORDER)
-    each(first_out, start)
-    drops_out, drops_in = block_copies(dsend, drecv, sd, rd, 1)
-    each(drops_out, start)
+    head_corners.start()
+    heads.start()
+    drops.start()
 
     khigh, klow = halves(
         jnp.concatenate([jnp.where(elane == e, tab[T_KT], 0.0) for e in range(EZ)], axis=0)
@@ -329,6 +340,9 @@
         both = both[:, 0:128] + both[:, 128:256]
         return [both[8 * i : 8 * i + 8, :] for i in range(8)]
 
+    def block_of(arrived, own, b):
+        return own.at[b] if b == DRIFT else arrived.at[AWAY.index(b)]
+
     def basis_block(b):
         def basis(r):
             value = tab[T_LAG]
@@ -336,7 +350,7 @@
                 value = value * jnp.where(sub == m, 1.0, r - float(NODES[m]))
             return value, turned(value, tab, T_DT)
 
-        tile = drecv.at[b] if b != DRIFT else dsend.at[b]
+        tile = block_of(drecv, dsend, b)
         eid = row_of(tile, 7)
         lx[b], dx[b] = basis(row_of(tile, 0))
         ly[b], dy[b] = basis(row_of(tile, 1))
@@ -376,11 +390,14 @@
 
     basis_block(DRIFT)
 
-    each(first_in, wait_recv)
-    residual = combine(rhs, lambda k: hrecv.at[k])
+    heads.wait()
+    head_corners.wait()
+    residual = combine(rhs, lambda n: hrecv[n, 0], lambda n: hcr[n, 0])
     factor = {(0, 0): amet}
-    for d in DIRS:
-        factor[(-d[0], -d[1])] = row_of(hrecv.at[SLOT[d]], 8)
+    for n, d in enumerate(FACES):
+        factor[(-d[0], -d[1])] = hrecv[n, 1]
+    for n, d in enumerate(CORNERS):
+        factor[(-d[0], -d[1])] = wide(hcr[n, 1])
     own_x = amet + edges(factor[(0, -1)], factor[(0, 1)])
     a_y = [amet + factor[(-1, 0)]] + [amet] * 6 + [amet + factor[(1, 0)]]
     side = {
@@ -410,9 +427,9 @@
     inv_diag, update = [], []
     for i in range(8):
         w_i, q_i = float(WEIGHTS[i]), float(QDIAG[i])
-        first, second = planes[i if i in planes else 1]
+        plane, mixed = planes[i if i in planes else 1]
         residual[i] = (w_i * wj) * residual[i]
-        diagonal = (q_i * wj + w_i * tab[T_QJ]) * first + (w_i * wj) * second
+        diagonal = (q_i * wj + w_i * tab[T_QJ]) * plane + (w_i * wj) * mixed
         inv_diag.append(1.0 / diagonal)
         update.append(inv_diag[i] * residual[i] * (1.0 / center))
     iterate = update
@@ -429,27 +446,6 @@
     for d in FACES:
         csend[COEF[d]] = across[d]
         csend[COEF[d] + 1] = inv_face[d]
-
-    def to_faces(source, recv, send_sems, recv_sems, dirs):
-        sent = [
-            pltpu.make_async_remote_copy(
-                src_ref=source(d),
-                dst_ref=recv.at[n],
-                send_sem=send_sems.at[n],
-                recv_sem=recv_sems.at[n],
-                device_id=device(*d),
-                device_id_type=MESH,
-            )
-            for n, d in enumerate(dirs)
-        ]
-        to = [exists(*d) for d in dirs]
-        of = [exists(-d[0], -d[1]) for d in dirs]
-        return list(zip(sent, to)), list(zip(sent, of))
-
-    def lines_of(u):
-        for i in range(8):
-            ub[8 * i : 8 * i + 8, :] = u[i]
-        return [ub[pl.ds(j, 8, stride=8), :] for j in range(8)]
 
     def ends(u, send, inner):
         lines = lines_of(u)
@@ -498,49 +494,32 @@
     def opposite(d):
         return (-d[0], -d[1])
 
-    ends(update, nsend.at[0], False)
-    near_out, near_in = to_faces(
-        lambda d: nsend.at[0, PLACE[d]], nrecv.at[0], s1.at[0], r1.at[0], FACES
-    )
-    each(near_out, start)
-    coef_out, coef_in = to_faces(lambda d: csend, crecv, sc, rc, FACES)
-    each(coef_out, start)
+    ends(update, first, False)
+    near_one.start()
     own = own_part(update)
     residual = [residual[i] - own[i] for i in range(8)]
-    each(drops_in, wait_recv)
+    coefs.start()
+    drops.wait()
     basis_block(1)
     basis_block(3)
-    each(near_in, wait_recv)
+    near_one.wait()
     residual = less_beside(residual, {opposite(d): nrecv[0, n] for n, d in enumerate(FACES)})
     update = advanced(update, residual, steps[0])
     iterate = [iterate[i] + update[i] for i in range(8)]
-    flights = [near_out, coef_out]
-
-    send = nsend.at[1]
-    ends(update, send, False)
-    send[4] = send[0]
-    far_out, far_in = to_faces(
-        lambda d: send.at[PLACE[(d[0] // 2, d[1] // 2)]],
-        farrecv, sf, rf, [(2 * x, 2 * y) for x, y in FACES],
-    )
-    corner_out, corner_in = to_faces(
-        lambda d: send.at[pl.ds(PAIR[d], 2)], crnrecv, sk, rk, CORNERS
-    )
-    near_out, near_in = to_faces(lambda d: send.at[PLACE[d]], nrecv.at[1], s1.at[1], r1.at[1], FACES)
-    each(far_out, start)
-    each(corner_out, start)
-    each(near_out, start)
+
+    ends(update, second, False)
+    second[4] = second[0]
+    near_two.start()
+    far_two.start()
     own = own_part(update)
     residual = [residual[i] - own[i] for i in range(8)]
     ends(advanced(update, residual, steps[1]), tsend, True)
-    tilde_out, tilde_in = to_faces(lambda d: tsend.at[PLACE[d]], trecv, st, rt, FACES)
-    each(tilde_out, start)
-    flights += [far_out, corner_out, near_out, tilde_out]
+    tilde.start()
     basis_block(0)
     basis_block(4)
     base_values()
 
-    each(near_in, wait_recv)
+    near_two.wait()
     residual = less_beside(residual, {opposite(d): nrecv[1, n] for n, d in enumerate(FACES)})
     update = advanced(update, residual, steps[1])
     iterate = [iterate[i] + update[i] for i in range(8)]
@@ -548,12 +527,12 @@
     own = own_part(update)
     residual = [residual[i] - own[i] for i in range(8)]
 
-    for arrived in (coef_in, far_in, corner_in, tilde_in):
-        each(arrived, wait_recv)
+    for group in (coefs, far_two, tilde):
+        group.wait()
 
     def from_corner(at, along):
         d = opposite(at)
-        return crnrecv[CORNERS.index(d), (PLACE[along] - PAIR[d]) % 4]
+        return grecv[4 + 2 * CORNERS.index(d) + (PLACE[along] - PAIR[d]) % 4]
 
     flow = {}
     for n, d in enumerate(FACES):
@@ -579,7 +558,7 @@
         else:
             shared = lines[0 if forward else 7]
         flow[at] = (
-            trecv[n] + far_weight * change(at, farrecv[n]) + edges(*rims) + near_weight * shared
+            trecv[n] + far_weight * change(at, grecv[n]) + edges(*rims) + near_weight * shared
         )
     residual = less_beside(residual, flow)
     update = advanced(update, residual, steps[2])
@@ -604,15 +583,14 @@
             contract(flat, lx.at[b], dy.at[b]),
             contract(slope, lx.at[b], ly.at[b]),
         ]
-        tile = drecv.at[b] if b != DRIFT else dsend.at[b]
+        tile = block_of(drecv, dsend, b)
         force = []
         for c in range(3):
             fluid = fbase[b, c : c + 1, :] - grads[c]
             rsend[b, c : c + 1, :] = fluid
             force.append(tile[6:7, :] * (tile[3 + c : 4 + c, :] - fluid))
         forces.append(force)
-    backs_out, backs_in = block_copies(rsend, rrecv, sr, rr, -1)
-    each(backs_out, start)
+    backs.start()
 
     columns_high, columns_low = [], []
     for b in range(REACH):
@@ -634,28 +612,35 @@
     for i in range(24):
         mb[8 * i : 8 * i + 8, :] = drag[i]
     for c in range(3):
-        fsend[0, c] = drag[8 * c + 7]
-        fsend[1, c] = drag[8 * c]
-        fsend[2, c] = mb[pl.ds(64 * c + 7, 8, stride=8), :]
-        fsend[3, c] = mb[pl.ds(64 * c, 8, stride=8), :]
-    last_out, last_in = copies(fsend, frecv, s4, r4, ORDER)
-    each(last_out, start)
-
-    each(backs_in, wait_recv)
+        for n, d in enumerate(CORNERS):
+            row = edge_row(d[1])
+            fcs[n, c] = drag[8 * c + edge_row(d[0])][row : row + 1, :]
+        for n, d in enumerate(FACES):
+            row = edge_row(d[0] + d[1])
+            if d[0]:
+                fsend[n, c] = drag[8 * c + row]
+            else:
+                fsend[n, c] = mb[pl.ds(64 * c + row, 8, stride=8), :]
+    tail_corners.start()
+    tails.start()
+
+    backs.wait()
     for b in range(REACH):
-        tile = rrecv.at[b] if b != DRIFT else rsend.at[b]
+        tile = block_of(rrecv, rsend, b)
         for c in range(3):
             accel = dprop[b, 0:1, :] * (tile[c : c + 1, :] - dvel[3 * b + c])
             acc_out[3 * b + c] = jnp.where(lane[0:1] < cnt[0, 0, b], accel, 0.0)
 
-    each(last_in, wait_recv)
+    tails.wait()
+    tail_corners.wait()
     for c in range(3):
-        value = combine(drag[8 * c : 8 * c + 8], lambda k: frecv.at[k, c])
+        value = combine(
+            drag[8 * c : 8 * c + 8], lambda n: frecv[n, c], lambda n: fcr[n, c]
+        )
         for i in range(8):
             m_out[c, i] = value[i]
 
-    for sent in [first_out, drops_out] + flights + [backs_out, last_out]:
-        each(sent, wait_send)
+    pltpu.make_async_copy(ledger, ledger, send_sems.at[0]).wait()
 
 
 def deliver(p_in, m_in, acc_in, p_out, m_out, acc_out, sems):
@@ -678,7 +663,14 @@
     dvel = dvel.reshape(REACH * 3, 1, CAP)
     dprop = dprop.reshape(REACH, 2, CAP)
     tile = (8, 128)
+    row = (1, 128)
     blocks = pltpu.VMEM((REACH,) + tile, F32)
+    arrive_shapes = [
+        (4, 2) + tile, (4, 2) + row, (4,) + tile, (4,) + tile, (4, 8) + tile, (4,) + tile,
+        (12,) + tile, (4,) + tile, (4,) + tile, (4, 3) + tile, (4, 3) + row,
+    ]
+    arrive = [pltpu.VMEM(shape, F32) for shape in arrive_shapes]
+    total_rows = sum(int(np.prod(shape)) for shape in arrive_shapes) // 128
     shapes = (
         jax.ShapeDtypeStruct((8, 8, 128), F32),
         jax.ShapeDtypeStruct((3, 8, 8, 128), F32),
@@ -712,41 +704,33 @@
             blocks,
             blocks,
             blocks,
-            pltpu.VMEM((4, 16, 128), F32),
-            pltpu.VMEM((8, 16, 128), F32),
+            pltpu.VMEM((4, 2) + tile, F32),
+            arrive[0],
+            pltpu.VMEM((4, 2) + row, F32),
+            arrive[1],
             pltpu.VMEM((2, 5) + tile, F32),
             pltpu.VMEM((2, 4) + tile, F32),
             pltpu.VMEM((4, 3) + tile, F32),
-            pltpu.VMEM((8, 3) + tile, F32),
+            arrive[9],
+            pltpu.VMEM((4, 3) + row, F32),
+            arrive[10],
             blocks,
+            arrive[2],
             blocks,
-            blocks,
-            blocks,
+            arrive[8],
             pltpu.VMEM((8,) + tile, F32),
-            pltpu.VMEM((4, 8) + tile, F32),
+            arrive[4],
             pltpu.VMEM((4,) + tile, F32),
-            pltpu.VMEM((4,) + tile, F32),
-            pltpu.VMEM((4,) + tile, F32),
-            pltpu.VMEM((4, 2) + tile, F32),
-            dma((9,)),
-            dma((8,)),
-            dma((8,)),
-            dma((2, 4)),
-            dma((2, 4)),
-            dma((8,)),
-            dma((8,)),
-            dma((REACH,)),
-            dma((REACH,)),
-            dma((REACH,)),
-            dma((REACH,)),
-            dma((4,)),
-            dma((4,)),
-            dma((4,)),
-            dma((4,)),
-            dma((4,)),
-            dma((4,)),
-            dma((4,)),
-            dma((4,)),
+            arrive[7],
+            arrive[6],
+            pltpu.VMEM((8,) + tile, F32),
+            pltpu.VMEM((3,) + row, F32),
+            *arrive,
+            pltpu.VMEM((total_rows,) + row, F32),
+            pltpu.VMEM((REACH * 9,) + row, F32),
+            dma((6,)),
+            dma((1,)),
+            dma((len(arrive),)),
         ],
         compiler_params=pltpu.CompilerParams(
             collective_id=0, has_side_effects=True, vmem_limit_bytes=32 * 1024 * 1024

time: 31.8 us -> 30.2 us (0.950)
  Pallas kernels: 31 us -> 29.4 us
    pallas_call x1, Pallas kernels: 30.3 us -> 28.7 us  [on_device(): pl.pallas_call(kernel, out_shape=shapes, in_specs=[hbm] * 9, out_specs=(v...]
where the time goes in v3:
time: 30.2 us; the launch traced here: 30 us
  Pallas kernels  29.4 us (97%)
  between operations  0.64 us (2%)
    pallas_call x1, Pallas kernels, on_device(): pl.pallas_call(kernel, out_shape=shapes, in_specs=[hbm] * 9, out_specs=(v...  28.7 us
    pallas_call x1, Pallas kernels, on_device(): pl.pallas_call(deliver, out_shape=shapes, in_specs=[vmem] * 3, out_specs=...  0.68 us

profile of v3, /device:TPU:7, one launch (start us, length us, event | category | flops | bytes accessed | tf_op | source)
XLA Modules:
  0.0 30.0 jit_solution(12005099446231132484)
XLA Ops:
  0.6 28.7 %shard_map.112 = (f32[8,8,128]{2,1,0:T(8,128)S(1)}, f32[3,8,8,128]{3,2,1,0:T(8,128)S(1)}, f32[15,1,128]{2,1,0:T(1,128)S(1)}) custom-call(f32[8,8,128]{2,1,0:T(8,128)} %src_h.1, f32[1,1,16]{2,1,0:T(1,128)} %met_h.1, f32[3,8,8,128]{3,2,1,0:T(8,128)} %bvel_h.1, s32[5,1,128]{2,1,0:T(1,128)} %bitcast.10, f32[15,1,128]{2,1,0:T(1,128)} %bitcast.7, ...), custom_call_target="tpu_custom_call" | custom-call | tf_op jit(solution)/shard_map/pallas_call | solution.py:681
  29.3 0.7 %shard_map.113 = (f32[8,8,128]{2,1,0:T(8,128)}, f32[3,8,8,128]{3,2,1,0:T(8,128)}, f32[15,1,128]{2,1,0:T(1,128)}) custom-call(f32[8,8,128]{2,1,0:T(8,128)S(1)} %get-tuple-element.9.p_in, f32[3,8,8,128]{3,2,1,0:T(8,128)S(1)} %get-tuple-element.10.m_in, f32[15,1,128]{2,1,0:T(1,128)S(1)} %get-tuple-element.11.acc_in), custom_call_target="tpu_custom_call" | custom-call | tf_op jit(solution)/shard_map/pallas_call | solution.py:739

commit v4 on v3

--- a/solution.py
+++ b/solution.py
@@ -29,11 +29,11 @@
 
 FACES = [(1, 0), (-1, 0), (0, 1), (0, -1)]
 CORNERS = [(1, 1), (1, -1), (-1, 1), (-1, -1)]
+FAR = [(2, 0), (-2, 0), (0, 2), (0, -2)]
+FAR_CORNERS = [(2, 1), (2, -1), (-2, 1), (-2, -1), (1, 2), (1, -2), (-1, 2), (-1, -2)]
 AWAY = [0, 4, 1, 3]
 PLACE = {(1, 0): 0, (0, 1): 1, (-1, 0): 2, (0, -1): 3}
 PAIR = {(1, 1): 0, (-1, 1): 1, (-1, -1): 2, (1, -1): 3}
-COEF = {(-1, 0): 0, (1, 0): 2, (0, -1): 4, (0, 1): 6}
-AWAY = [0, 4, 1, 3]
 
 
 def legendre_seven(points):
@@ -66,7 +66,7 @@
 
 PACKED = 5
 T_WK, T_QK, T_KT, T_ZM, T_WJ, T_QJ, T_CY, T_DT, T_LAG, T_END = 0, 1, 2, 3, 4, 5, 6, 14, 22, 23
-TILES = 25
+TILES = 27
 
 
 def constant_tiles():
@@ -89,6 +89,8 @@
     columns[:, T_LAG] = 1.0 / gaps.prod(1)
     columns[0:7, T_END] = STIFF[7, 0:7]
     columns[1:8, T_END + 1] = STIFF[0, 1:8]
+    columns[1:7, T_END + 2] = STIFF[7, 1:7]
+    columns[1:7, T_END + 3] = STIFF[0, 1:7]
     return tiles.astype(np.float32)
 
 
@@ -139,8 +141,8 @@
     p_out, m_out, acc_out,
     src, met, bvel, elem, coord, dvel, dprop, cnt, pack, tab,
     ub, mb, kz, lz, ld, lx, dx, ly, dy, fbase,
-    hsend, hrecv, hcs, hcr, nsend, nrecv, fsend, frecv, fcs, fcr,
-    dsend, drecv, rsend, rrecv, csend, crecv, tsend, trecv, grecv, zeros, zero_rows,
+    hsend, hrecv, hcs, hcr, hfr, hrs, hrr, nsend, nrecv, fsend, frecv, fcs, fcr,
+    dsend, drecv, rsend, rrecv, tsend, trecv, grecv, zeros, zero_rows,
     *rest,
 ):
     *spare, ledger, load_ledger, si, send_sems, recv_sems = rest
@@ -202,7 +204,7 @@
                 )
 
     barrier = pltpu.get_barrier_semaphore()
-    partners = FACES + CORNERS + [(2, 0), (-2, 0), (0, 2), (0, -2)]
+    partners = FACES + CORNERS + FAR + FAR_CORNERS
     greeted = jnp.int32(0)
     for d in partners:
         there = exists(*d)
@@ -250,31 +252,67 @@
     def edge_row(d):
         return 7 if d > 0 else 0
 
+    def ends(u, group_range):
+        lines = lines_of(u)
+        return {
+            d: total(float(STIFF[row, m]) * group[m] for m in group_range(row))
+            for d, group, row in (
+                ((1, 0), u, 7), ((-1, 0), u, 0), ((0, 1), lines, 7), ((0, -1), lines, 0)
+            )
+        }
+
+    def opposite(d):
+        return (-d[0], -d[1])
+
+    center = (UPPER_BOUND + LOWER_BOUND) / 2.0
+    half_width = (UPPER_BOUND - LOWER_BOUND) / 2.0
+    bound = center / half_width
+    rho = 1.0 / bound
+    qk, qj = tab[T_QK], tab[T_QJ]
+    plane, mixed = sum_z(wk * amet), sum_z(qk * amet + wk)
+    early = []
+    for i in range(8):
+        w_i, q_i = float(WEIGHTS[i]), float(QDIAG[i])
+        diagonal = (q_i * wj + w_i * qj) * plane + (w_i * wj) * mixed
+        early.append((w_i / center) * (wj * rhs[i]) / diagonal)
+    middle = ends(early, lambda row: range(1, 7))
+
     lines = lines_of(rhs)
+    skin = {d: (rhs if d[0] else lines)[edge_row(d[0] + d[1])] for d in FACES}
     for n, d in enumerate(FACES):
-        hsend[n, 0] = (rhs if d[0] else lines)[edge_row(d[0] + d[1])]
-        hsend[n, 1] = amet
+        for f in FACES:
+            hsend[n, PLACE[f]] = skin[f]
+        hsend[n, 4] = jnp.where(top, amet, middle[d])
+        hrs[n, 0] = amet[0:1, :]
+        hrs[n, 1] = amet[0:1, :]
     for n, d in enumerate(CORNERS):
-        row = edge_row(d[1])
-        hcs[n, 0] = rhs[edge_row(d[0])][row : row + 1, :]
-        hcs[n, 1] = amet[0:1, :]
+        hcs[n, 0] = skin[(d[0], 0)]
+        hcs[n, 1] = jnp.where(sub == edge_row(d[0]), amet, skin[(0, d[1])])
+    for n, d in enumerate(FAR_CORNERS):
+        if abs(d[0]) == 2:
+            face, row = skin[(d[0] // 2, 0)], edge_row(d[1])
+        else:
+            face, row = skin[(0, d[1] // 2)], edge_row(d[0])
+        hrs[4 + n, 0] = face[row : row + 1, :]
+        hrs[4 + n, 1] = amet[0:1, :]
 
     def slots(dirs, source):
         return [(d, source(n, d), n) for n, d in enumerate(dirs)]
 
     blocks_to = [((b - DRIFT, 0), dsend.at[b], n) for n, b in enumerate(AWAY)]
     blocks_back = [((DRIFT - b, 0), rsend.at[b], n) for n, b in enumerate(AWAY)]
-    first, second = nsend.at[0], nsend.at[1]
     heads = Group(hrecv, slots(FACES, lambda n, d: hsend.at[n]))
     head_corners = Group(hcr, slots(CORNERS, lambda n, d: hcs.at[n]))
+    head_far = Group(
+        hfr, [(d, hsend.at[0, PLACE[(d[0] // 2, d[1] // 2)]], n) for n, d in enumerate(FAR)]
+    )
+    head_rows = Group(hrr, slots(FAR + FAR_CORNERS, lambda n, d: hrs.at[n]))
     drops = Group(drecv, blocks_to)
-    near_one = Group(nrecv.at[0], slots(FACES, lambda n, d: first.at[PLACE[d]]))
-    coefs = Group(crecv, slots(FACES, lambda n, d: csend))
-    near_two = Group(nrecv.at[1], slots(FACES, lambda n, d: second.at[PLACE[d]]))
+    near_two = Group(nrecv, slots(FACES, lambda n, d: nsend.at[PLACE[d]]))
     far_two = Group(
         grecv,
-        [((2 * d[0], 2 * d[1]), second.at[PLACE[d]], n) for n, d in enumerate(FACES)]
-        + [(d, second.at[pl.ds(PAIR[d], 2)], pl.ds(4 + 2 * n, 2)) for n, d in enumerate(CORNERS)],
+        [(d, nsend.at[PLACE[(d[0] // 2, d[1] // 2)]], n) for n, d in enumerate(FAR)]
+        + [(d, nsend.at[pl.ds(PAIR[d], 2)], pl.ds(4 + 2 * n, 2)) for n, d in enumerate(CORNERS)],
     )
     tilde = Group(trecv, slots(FACES, lambda n, d: tsend.at[PLACE[d]]))
     backs = Group(rrecv, blocks_back)
@@ -320,6 +358,8 @@
     stage_drops()
 
     pl.semaphore_wait(barrier, greeted)
+    head_rows.start()
+    head_far.start()
     head_corners.start()
     heads.start()
     drops.start()
@@ -390,14 +430,28 @@
 
     basis_block(DRIFT)
 
-    heads.wait()
-    head_corners.wait()
-    residual = combine(rhs, lambda n: hrecv[n, 0], lambda n: hcr[n, 0])
-    factor = {(0, 0): amet}
+    for group in (heads, head_corners, head_far, head_rows):
+        group.wait()
+    skins, factor, middle_of = {}, {(0, 0): amet}, {}
     for n, d in enumerate(FACES):
-        factor[(-d[0], -d[1])] = hrecv[n, 1]
+        at = opposite(d)
+        skins[at] = {f: hrecv[n, PLACE[f]] for f in FACES}
+        middle_of[at] = hrecv[n, 4]
+        factor[at] = wide(middle_of[at][0:1, :])
     for n, d in enumerate(CORNERS):
-        factor[(-d[0], -d[1])] = wide(hcr[n, 1])
+        row = edge_row(d[0])
+        skins[opposite(d)] = {(d[0], 0): hcr[n, 0], (0, d[1]): hcr[n, 1]}
+        factor[opposite(d)] = wide(hcr[n, 1, row : row + 1, :])
+    point = {}
+    for n, d in enumerate(FAR + FAR_CORNERS):
+        point[opposite(d)] = wide(hrr[n, 0])
+        factor[opposite(d)] = wide(hrr[n, 1])
+
+    def shared_row(n):
+        row = edge_row(CORNERS[n][1])
+        return hcr[n, 0, row : row + 1, :]
+
+    residual = combine(rhs, lambda n: skins[opposite(FACES[n])][FACES[n]], shared_row)
     own_x = amet + edges(factor[(0, -1)], factor[(0, 1)])
     a_y = [amet + factor[(-1, 0)]] + [amet] * 6 + [amet + factor[(1, 0)]]
     side = {
@@ -414,48 +468,22 @@
     count_y = 1.0 + edges(present(0, -1), present(0, 1))
     count_x = [1.0 + present(-1, 0)] + [1.0] * 6 + [1.0 + present(1, 0)]
 
-    center = (UPPER_BOUND + LOWER_BOUND) / 2.0
-    half_width = (UPPER_BOUND - LOWER_BOUND) / 2.0
-    bound = center / half_width
-    rho = 1.0 / bound
-
     wkj = wk * wj
     mass = [wkj * (count_x[i] * count_y) for i in range(8)]
     planes = {}
     for i in (0, 1, 7):
-        planes[i] = (sum_z(wk * a_sum[i]), sum_z(tab[T_QK] * a_sum[i] + wk * (count_x[i] * count_y)))
+        planes[i] = (sum_z(wk * a_sum[i]), sum_z(qk * a_sum[i] + wk * (count_x[i] * count_y)))
     inv_diag, update = [], []
     for i in range(8):
         w_i, q_i = float(WEIGHTS[i]), float(QDIAG[i])
         plane, mixed = planes[i if i in planes else 1]
         residual[i] = (w_i * wj) * residual[i]
-        diagonal = (q_i * wj + w_i * tab[T_QJ]) * plane + (w_i * wj) * mixed
+        diagonal = (q_i * wj + w_i * qj) * plane + (w_i * wj) * mixed
         inv_diag.append(1.0 / diagonal)
         update.append(inv_diag[i] * residual[i] * (1.0 / center))
     iterate = update
 
     across = {d: wkj * side[d] for d in FACES}
-    for i in range(8):
-        mb[8 * i : 8 * i + 8, :] = inv_diag[i]
-    inv_face = {
-        (-1, 0): inv_diag[0],
-        (1, 0): inv_diag[7],
-        (0, -1): mb[pl.ds(0, 8, stride=8), :],
-        (0, 1): mb[pl.ds(7, 8, stride=8), :],
-    }
-    for d in FACES:
-        csend[COEF[d]] = across[d]
-        csend[COEF[d] + 1] = inv_face[d]
-
-    def ends(u, send, inner):
-        lines = lines_of(u)
-        for d, group, row in (
-            ((1, 0), u, 7), ((-1, 0), u, 0), ((0, 1), lines, 7), ((0, -1), lines, 0)
-        ):
-            send[PLACE[d]] = total(
-                float(STIFF[row, m]) * group[m] for m in range(8) if not (inner and m == row)
-            )
-
     def own_part(u):
         flat, slope = along_z(u), stiff_x(u)
         out = []
@@ -491,43 +519,98 @@
     def advanced(u, left, step):
         return [step[0] * u[i] + step[1] * (inv_diag[i] * left[i]) for i in range(8)]
 
-    def opposite(d):
-        return (-d[0], -d[1])
-
-    ends(update, first, False)
-    near_one.start()
+    def outer(value, a_near, count):
+        w_0, q_0 = float(WEIGHTS[0]), float(QDIAG[0])
+        diagonal = (q_0 * wj + w_0 * qj) * sum_z(wk * a_near) + (w_0 * wj) * sum_z(
+            qk * a_near + wk * jnp.maximum(count, 1.0)
+        )
+        inverse = 1.0 / diagonal
+        return inverse, inverse * (((w_0 / center) * wj) * value)
+
+    def plus(p, q):
+        return (p[0] + q[0], p[1] + q[1])
+
+    def rim_of(d, t):
+        return (0, t) if d[0] else (t, 0)
+
+    def ordered(at, far, near):
+        return edges(far, near) if at[0] + at[1] < 0 else edges(near, far)
+
+    def a_of(*places):
+        return total(factor[p] for p in places)
+
+    def n_of(*places):
+        return total(present(*p) for p in places)
+
+    shell, flow = {}, {}
+    lines = lines_of(update)
+    for n, d in enumerate(FACES):
+        at = opposite(d)
+        far = plus(at, at)
+        forward = d[0] + d[1] > 0
+        beside = {t: plus(at, rim_of(d, t)) for t in (-1, 1)}
+        beyond = {t: plus(far, rim_of(d, t)) for t in (-1, 1)}
+        row = edge_row(at[0] + at[1])
+        corner_values = [
+            wide(skins[beside[t]][opposite(rim_of(d, t))][row : row + 1, :]) + point[beyond[t]]
+            for t in (-1, 1)
+        ]
+        inverse, value = outer(
+            skins[at][at] + hfr[n] + edges(*corner_values),
+            a_of(at, far) + edges(*[a_of(beside[t], beyond[t]) for t in (-1, 1)]),
+            n_of(at, far) + edges(*[n_of(beside[t], beyond[t]) for t in (-1, 1)]),
+        )
+        weight = wkj * (factor[far] + edges(factor[beyond[-1]], factor[beyond[1]]))
+        shell[at, at] = (weight, inverse)
+        sums = []
+        for t in (-1, 1):
+            rim = rim_of(d, t)
+            inverse, rim_value = outer(
+                skins[at][rim] + skins[beside[t]][opposite(rim)],
+                a_of(at, beside[t]) + ordered(at, a_of(far, beyond[t]), a_of((0, 0), rim)),
+                n_of(at, beside[t]) + ordered(at, n_of(far, beyond[t]), n_of((0, 0), rim)),
+            )
+            weight = wkj * (factor[beside[t]] + ordered(at, factor[beyond[t]], factor[rim]))
+            shell[at, rim] = (weight, inverse)
+            weights = tab[T_END + (2 if forward else 3)]
+            sums.append(wide(jnp.sum(weights * rim_value, axis=0, keepdims=True)))
+        far_weight = float(STIFF[7, 0] if forward else STIFF[0, 7])
+        near_weight = float(STIFF[7, 7] if forward else STIFF[0, 0])
+        shared = (update if d[0] else lines)[0 if forward else 7]
+        inner = jnp.where(top, sums[0], jnp.where(bottom, sums[1], middle_of[at]))
+        flow[at] = inner + far_weight * value + near_weight * shared
+
     own = own_part(update)
-    residual = [residual[i] - own[i] for i in range(8)]
-    coefs.start()
-    drops.wait()
-    basis_block(1)
-    basis_block(3)
-    near_one.wait()
-    residual = less_beside(residual, {opposite(d): nrecv[0, n] for n, d in enumerate(FACES)})
+    residual = less_beside([residual[i] - own[i] for i in range(8)], flow)
     update = advanced(update, residual, steps[0])
     iterate = [iterate[i] + update[i] for i in range(8)]
 
-    ends(update, second, False)
-    second[4] = second[0]
+    for d, tile in ends(update, lambda row: range(8)).items():
+        nsend[PLACE[d]] = tile
+        if PLACE[d] == 0:
+            nsend[4] = tile
     near_two.start()
     far_two.start()
     own = own_part(update)
     residual = [residual[i] - own[i] for i in range(8)]
-    ends(advanced(update, residual, steps[1]), tsend, True)
+    guess = advanced(update, residual, steps[1])
+    for d, tile in ends(guess, lambda row: range(7) if row else range(1, 8)).items():
+        tsend[PLACE[d]] = tile
     tilde.start()
-    basis_block(0)
-    basis_block(4)
+    drops.wait()
+    for b in AWAY:
+        basis_block(b)
     base_values()
 
     near_two.wait()
-    residual = less_beside(residual, {opposite(d): nrecv[1, n] for n, d in enumerate(FACES)})
+    residual = less_beside(residual, {opposite(d): nrecv[n] for n, d in enumerate(FACES)})
     update = advanced(update, residual, steps[1])
     iterate = [iterate[i] + update[i] for i in range(8)]
     lines = lines_of(update)
     own = own_part(update)
     residual = [residual[i] - own[i] for i in range(8)]
 
-    for group in (coefs, far_two, tilde):
+    for group in (far_two, tilde):
         group.wait()
 
     def from_corner(at, along):
@@ -537,11 +620,10 @@
     flow = {}
     for n, d in enumerate(FACES):
         at = opposite(d)
-        coef = crecv.at[n]
 
         def change(face, across_it):
-            spread = sum_z(coef[COEF[face]] * across_it)
-            return (-steps[1][1]) * (coef[COEF[face] + 1] * spread)
+            weight, inverse = shell[at, face]
+            return (-steps[1][1]) * (inverse * sum_z(weight * across_it))
 
         forward = d[0] + d[1] > 0
         far_weight = float(STIFF[7, 0] if forward else STIFF[0, 7])
@@ -549,8 +631,8 @@
         weights = tab[T_END if forward else T_END + 1]
         rims = []
         for t in (-1, 1):
-            rim = (0, t) if d[0] else (t, 0)
-            corner = (at[0] + rim[0], at[1] + rim[1])
+            rim = rim_of(d, t)
+            corner = plus(at, rim)
             changed = change(rim, from_corner(corner, opposite(rim)))
             rims.append(wide(jnp.sum(weights * changed, axis=0, keepdims=True)))
         if d[0]:
@@ -666,7 +748,7 @@
     row = (1, 128)
     blocks = pltpu.VMEM((REACH,) + tile, F32)
     arrive_shapes = [
-        (4, 2) + tile, (4, 2) + row, (4,) + tile, (4,) + tile, (4, 8) + tile, (4,) + tile,
+        (4, 5) + tile, (4, 2) + tile, (4,) + tile, (12, 2) + row, (4,) + tile, (4,) + tile,
         (12,) + tile, (4,) + tile, (4,) + tile, (4, 3) + tile, (4, 3) + row,
     ]
     arrive = [pltpu.VMEM(shape, F32) for shape in arrive_shapes]
@@ -704,22 +786,23 @@
             blocks,
             blocks,
             blocks,
+            pltpu.VMEM((4, 5) + tile, F32),
+            arrive[0],
             pltpu.VMEM((4, 2) + tile, F32),
-            arrive[0],
-            pltpu.VMEM((4, 2) + row, F32),
             arrive[1],
-            pltpu.VMEM((2, 5) + tile, F32),
-            pltpu.VMEM((2, 4) + tile, F32),
+            arrive[2],
+            pltpu.VMEM((12, 2) + row, F32),
+            arrive[3],
+            pltpu.VMEM((5,) + tile, F32),
+            arrive[5],
             pltpu.VMEM((4, 3) + tile, F32),
             arrive[9],
             pltpu.VMEM((4, 3) + row, F32),
             arrive[10],
             blocks,
-            arrive[2],
+            arrive[4],
             blocks,
             arrive[8],
-            pltpu.VMEM((8,) + tile, F32),
-            arrive[4],
             pltpu.VMEM((4,) + tile, F32),
             arrive[7],
             arrive[6],

time: 30.2 us -> 27.2 us (0.901)
  Pallas kernels: 29.4 us -> 26.5 us
    pallas_call x1, Pallas kernels: 28.7 us -> 25.8 us  [on_device(): pl.pallas_call(kernel, out_shape=shapes, in_specs=[hbm] * 9, out_specs=(v...]
where the time goes in v4:
time: 27.2 us; the launch traced here: 27.1 us
  Pallas kernels  26.5 us (97%)
  between operations  0.64 us (2%)
    pallas_call x1, Pallas kernels, on_device(): pl.pallas_call(kernel, out_shape=shapes, in_specs=[hbm] * 9, out_specs=(v...  25.8 us
    pallas_call x1, Pallas kernels, on_device(): pl.pallas_call(deliver, out_shape=shapes, in_specs=[vmem] * 3, out_specs=...  0.68 us

profile of v4, /device:TPU:7, one launch (start us, length us, event | category | flops | bytes accessed | tf_op | source)
XLA Modules:
  0.0 27.1 jit_solution(9143343979925235746)
XLA Ops:
  0.6 25.8 %shard_map.112 = (f32[8,8,128]{2,1,0:T(8,128)S(1)}, f32[3,8,8,128]{3,2,1,0:T(8,128)S(1)}, f32[15,1,128]{2,1,0:T(1,128)S(1)}) custom-call(f32[8,8,128]{2,1,0:T(8,128)} %src_h.1, f32[1,1,16]{2,1,0:T(1,128)} %met_h.1, f32[3,8,8,128]{3,2,1,0:T(8,128)} %bvel_h.1, s32[5,1,128]{2,1,0:T(1,128)} %bitcast.10, f32[15,1,128]{2,1,0:T(1,128)} %bitcast.7, ...), custom_call_target="tpu_custom_call" | custom-call | tf_op jit(solution)/shard_map/pallas_call | solution.py:763
  26.4 0.7 %shard_map.113 = (f32[8,8,128]{2,1,0:T(8,128)}, f32[3,8,8,128]{3,2,1,0:T(8,128)}, f32[15,1,128]{2,1,0:T(1,128)}) custom-call(f32[8,8,128]{2,1,0:T(8,128)S(1)} %get-tuple-element.9.p_in, f32[3,8,8,128]{3,2,1,0:T(8,128)S(1)} %get-tuple-element.10.m_in, f32[15,1,128]{2,1,0:T(1,128)S(1)} %get-tuple-element.11.acc_in), custom_call_target="tpu_custom_call" | custom-call | tf_op jit(solution)/shard_map/pallas_call | solution.py:822

commit v5 on v4

--- a/solution.py
+++ b/solution.py
@@ -140,7 +140,7 @@
     src_h, met_h, bvel_h, elem_h, coord_h, dvel_h, dprop_h, cnt_h, tab_h,
     p_out, m_out, acc_out,
     src, met, bvel, elem, coord, dvel, dprop, cnt, pack, tab,
-    ub, mb, kz, lz, ld, lx, dx, ly, dy, fbase,
+    ub, mb, kz, lzd, lzt, lx, dx, ly, dy, fbase,
     hsend, hrecv, hcs, hcr, hfr, hrs, hrr, nsend, nrecv, fsend, frecv, fcs, fcr,
     dsend, drecv, rsend, rrecv, tsend, trecv, grecv, zeros, zero_rows,
     *rest,
@@ -204,7 +204,7 @@
                 )
 
     barrier = pltpu.get_barrier_semaphore()
-    partners = FACES + CORNERS + FAR + FAR_CORNERS
+    partners = FAR_CORNERS + FAR + CORNERS + FACES
     greeted = jnp.int32(0)
     for d in partners:
         there = exists(*d)
@@ -394,14 +394,17 @@
         eid = row_of(tile, 7)
         lx[b], dx[b] = basis(row_of(tile, 0))
         ly[b], dy[b] = basis(row_of(tile, 1))
-        span = slice(b * CAP, b * CAP + CAP)
-        for part, ref in zip(basis(row_of(tile, 2)), (lz, ld)):
+        for side_by, part in enumerate(basis(row_of(tile, 2))):
             high = part.astype(BF16).astype(F32)
             for piece, first in ((high, 0), (part - high, 128)):
                 spread = jnp.concatenate(
                     [jnp.where(eid == float(e), piece, 0.0) for e in range(EZ)], axis=0
                 )
-                ref[first : first + 128, span] = spread.astype(BF16)
+                spread = spread.astype(BF16)
+                start = (2 * b + side_by) * CAP
+                lzd[first : first + 128, start : start + CAP] = spread
+                if not side_by:
+                    lzt[b * CAP : b * CAP + CAP, first : first + 128] = jnp.transpose(spread)
 
     def contract(planes, first, second):
         inner = total(row_of(first, i) * planes[i] for i in range(8))
@@ -421,8 +424,8 @@
         loads[8].wait()
         left = stacked(jnp.concatenate([bvel[c, i] for c in range(3) for i in range(8)], axis=0))
         for b in range(REACH):
-            span = slice(b * CAP, b * CAP + CAP)
-            both = jnp.dot(left, lz[:, span], preferred_element_type=F32)
+            span = slice(2 * b * CAP, 2 * b * CAP + CAP)
+            both = jnp.dot(left, lzd[:, span], preferred_element_type=F32)
             both = both[0:192, :] + both[192:384, :]
             for c in range(3):
                 planes = [both[64 * c + 8 * i : 64 * c + 8 * i + 8, :] for i in range(8)]
@@ -652,14 +655,11 @@
     left = stacked(jnp.concatenate([amet * iterate[i] for i in range(8)], axis=0))
     forces = []
     for b in range(REACH):
-        span = slice(b * CAP, b * CAP + CAP)
-
-        def planes_of(ref):
-            both = jnp.dot(left, ref[:, span], preferred_element_type=F32)
-            both = both[0:64, :] + both[64:128, :]
-            return [both[8 * i : 8 * i + 8, :] for i in range(8)]
-
-        flat, slope = planes_of(lz), planes_of(ld)
+        span = slice(2 * b * CAP, 2 * b * CAP + 2 * CAP)
+        both = jnp.dot(left, lzd[:, span], preferred_element_type=F32)
+        both = both[0:64, :] + both[64:128, :]
+        flat = [both[8 * i : 8 * i + 8, 0:CAP] for i in range(8)]
+        slope = [both[8 * i : 8 * i + 8, CAP : 2 * CAP] for i in range(8)]
         grads = [
             contract(flat, dx.at[b], ly.at[b]),
             contract(flat, lx.at[b], dy.at[b]),
@@ -669,7 +669,7 @@
         force = []
         for c in range(3):
             fluid = fbase[b, c : c + 1, :] - grads[c]
-            rsend[b, c : c + 1, :] = fluid
+            rsend[b, c] = fluid
             force.append(tile[6:7, :] * (tile[3 + c : 4 + c, :] - fluid))
         forces.append(force)
     backs.start()
@@ -686,31 +686,37 @@
     left = jnp.concatenate(
         [jnp.concatenate(columns_high, axis=1), jnp.concatenate(columns_low, axis=1)], axis=0
     )
-    both = lax.dot_general(
-        left, lz[...], (((1,), (1,)), ((), ())), preferred_element_type=F32
-    )
+    both = jnp.dot(left, lzt[...], preferred_element_type=F32)
     drag = both[0:192, 0:128] + both[0:192, 128:256] + both[192:384, 0:128]
-    drag = [sum_z(drag[8 * i : 8 * i + 8, :]) for i in range(24)]
+    drag = [drag[8 * i : 8 * i + 8, :] for i in range(24)]
+    for c in range(3):
+        for i in (0, 7):
+            drag[8 * c + i] = sum_z(drag[8 * c + i])
     for i in range(24):
         mb[8 * i : 8 * i + 8, :] = drag[i]
     for c in range(3):
         for n, d in enumerate(CORNERS):
             row = edge_row(d[1])
             fcs[n, c] = drag[8 * c + edge_row(d[0])][row : row + 1, :]
+    tail_corners.start()
+    for c in range(3):
         for n, d in enumerate(FACES):
             row = edge_row(d[0] + d[1])
             if d[0]:
                 fsend[n, c] = drag[8 * c + row]
             else:
-                fsend[n, c] = mb[pl.ds(64 * c + row, 8, stride=8), :]
-    tail_corners.start()
+                line = mb[pl.ds(64 * c + row, 8, stride=8), :]
+                fsend[n, c] = jnp.where(top | bottom, line, sum_z(line))
     tails.start()
+    for c in range(3):
+        for i in range(1, 7):
+            drag[8 * c + i] = sum_z(drag[8 * c + i])
 
     backs.wait()
     for b in range(REACH):
         tile = block_of(rrecv, rsend, b)
         for c in range(3):
-            accel = dprop[b, 0:1, :] * (tile[c : c + 1, :] - dvel[3 * b + c])
+            accel = dprop[b, 0:1, :] * (tile[c] - dvel[3 * b + c])
             acc_out[3 * b + c] = jnp.where(lane[0:1] < cnt[0, 0, b], accel, 0.0)
 
     tails.wait()
@@ -749,7 +755,7 @@
     blocks = pltpu.VMEM((REACH,) + tile, F32)
     arrive_shapes = [
         (4, 5) + tile, (4, 2) + tile, (4,) + tile, (12, 2) + row, (4,) + tile, (4,) + tile,
-        (12,) + tile, (4,) + tile, (4,) + tile, (4, 3) + tile, (4, 3) + row,
+        (12,) + tile, (4,) + tile, (4, 3) + row, (4, 3) + tile, (4, 3) + row,
     ]
     arrive = [pltpu.VMEM(shape, F32) for shape in arrive_shapes]
     total_rows = sum(int(np.prod(shape)) for shape in arrive_shapes) // 128
@@ -779,8 +785,8 @@
             pltpu.VMEM((64, 128), F32),
             pltpu.VMEM((192, 128), F32),
             pltpu.VMEM((256, 256), BF16),
-            pltpu.VMEM((256, REACH * CAP), BF16),
-            pltpu.VMEM((256, REACH * CAP), BF16),
+            pltpu.VMEM((256, 2 * REACH * CAP), BF16),
+            pltpu.VMEM((REACH * CAP, 256), BF16),
             blocks,
             blocks,
             blocks,
@@ -801,7 +807,7 @@
             arrive[10],
             blocks,
             arrive[4],
-            blocks,
+            pltpu.VMEM((REACH, 3) + row, F32),
             arrive[8],
             pltpu.VMEM((4,) + tile, F32),
             arrive[7],

time: 27.2 us -> 27 us (level)
  Pallas kernels: 26.5 us -> 26.2 us
where the time goes in v5:
time: 27 us; the launch traced here: 26.8 us
  Pallas kernels  26.2 us (97%)
  between operations  0.64 us (2%)
    pallas_call x1, Pallas kernels, on_device(): pl.pallas_call(kernel, out_shape=shapes, in_specs=[hbm] * 9, out_specs=(v...  25.5 us
    pallas_call x1, Pallas kernels, on_device(): pl.pallas_call(deliver, out_shape=shapes, in_specs=[vmem] * 3, out_specs=...  0.68 us

profile of v5, /device:TPU:7, one launch (start us, length us, event | category | flops | bytes accessed | tf_op | source)
XLA Modules:
  0.0 26.8 jit_solution(14584535899399227373)
XLA Ops:
  0.6 25.5 %shard_map.112 = (f32[8,8,128]{2,1,0:T(8,128)S(1)}, f32[3,8,8,128]{3,2,1,0:T(8,128)S(1)}, f32[15,1,128]{2,1,0:T(1,128)S(1)}) custom-call(f32[8,8,128]{2,1,0:T(8,128)} %src_h.1, f32[1,1,16]{2,1,0:T(1,128)} %met_h.1, f32[3,8,8,128]{3,2,1,0:T(8,128)} %bvel_h.1, s32[5,1,128]{2,1,0:T(1,128)} %bitcast.10, f32[15,1,128]{2,1,0:T(1,128)} %bitcast.7, ...), custom_call_target="tpu_custom_call" | custom-call | tf_op jit(solution)/shard_map/pallas_call | solution.py:769
  26.2 0.7 %shard_map.113 = (f32[8,8,128]{2,1,0:T(8,128)}, f32[3,8,8,128]{3,2,1,0:T(8,128)}, f32[15,1,128]{2,1,0:T(1,128)}) custom-call(f32[8,8,128]{2,1,0:T(8,128)S(1)} %get-tuple-element.9.p_in, f32[3,8,8,128]{3,2,1,0:T(8,128)S(1)} %get-tuple-element.10.m_in, f32[15,1,128]{2,1,0:T(1,128)S(1)} %get-tuple-element.11.acc_in), custom_call_target="tpu_custom_call" | custom-call | tf_op jit(solution)/shard_map/pallas_call | solution.py:828

commit v6 on v5

--- a/solution.py
+++ b/solution.py
@@ -252,8 +252,8 @@
     def edge_row(d):
         return 7 if d > 0 else 0
 
-    def ends(u, group_range):
-        lines = lines_of(u)
+    def ends(u, group_range, lines=None):
+        lines = lines or lines_of(u)
         return {
             d: total(float(STIFF[row, m]) * group[m] for m in group_range(row))
             for d, group, row in (
@@ -487,15 +487,17 @@
     iterate = update
 
     across = {d: wkj * side[d] for d in FACES}
-    def own_part(u):
+    def own_part(u, lines):
         flat, slope = along_z(u), stiff_x(u)
+        for j, tile in enumerate(stiff_x(lines)):
+            mb[pl.ds(j, 8, stride=8), :] = tile
         out = []
         for i in range(8):
             w_i = float(WEIGHTS[i])
             out.append(
                 sum_z(
                     wkj * own_x * slope[i]
-                    + (w_i * wk) * a_y[i] * turned(u[i], tab, T_CY)
+                    + (w_i * wk) * a_y[i] * mb[8 * i : 8 * i + 8, :]
                     + (w_i * wj) * a_sum[i] * flat[i]
                     + w_i * mass[i] * u[i]
                 )
@@ -583,18 +585,19 @@
         inner = jnp.where(top, sums[0], jnp.where(bottom, sums[1], middle_of[at]))
         flow[at] = inner + far_weight * value + near_weight * shared
 
-    own = own_part(update)
+    own = own_part(update, lines)
     residual = less_beside([residual[i] - own[i] for i in range(8)], flow)
     update = advanced(update, residual, steps[0])
     iterate = [iterate[i] + update[i] for i in range(8)]
 
-    for d, tile in ends(update, lambda row: range(8)).items():
+    lines = lines_of(update)
+    for d, tile in ends(update, lambda row: range(8), lines).items():
         nsend[PLACE[d]] = tile
         if PLACE[d] == 0:
             nsend[4] = tile
     near_two.start()
     far_two.start()
-    own = own_part(update)
+    own = own_part(update, lines)
     residual = [residual[i] - own[i] for i in range(8)]
     guess = advanced(update, residual, steps[1])
     for d, tile in ends(guess, lambda row: range(7) if row else range(1, 8)).items():
@@ -610,7 +613,7 @@
     update = advanced(update, residual, steps[1])
     iterate = [iterate[i] + update[i] for i in range(8)]
     lines = lines_of(update)
-    own = own_part(update)
+    own = own_part(update, lines)
     residual = [residual[i] - own[i] for i in range(8)]
 
     for group in (far_two, tilde):

time: 27 us -> 27 us (level)
  no operation moved by 1% of the time
where the time goes in v6:
time: 27 us; the launch traced here: 26.8 us
  Pallas kernels  26.2 us (97%)
  between operations  0.64 us (2%)
    pallas_call x1, Pallas kernels, on_device(): pl.pallas_call(kernel, out_shape=shapes, in_specs=[hbm] * 9, out_specs=(v...  25.5 us
    pallas_call x1, Pallas kernels, on_device(): pl.pallas_call(deliver, out_shape=shapes, in_specs=[vmem] * 3, out_specs=...  0.68 us

profile of v6, /device:TPU:7, one launch (start us, length us, event | category | flops | bytes accessed | tf_op | source)
XLA Modules:
  0.0 26.8 jit_solution(2321787256919666042)
XLA Ops:
  0.6 25.5 %shard_map.112 = (f32[8,8,128]{2,1,0:T(8,128)S(1)}, f32[3,8,8,128]{3,2,1,0:T(8,128)S(1)}, f32[15,1,128]{2,1,0:T(1,128)S(1)}) custom-call(f32[8,8,128]{2,1,0:T(8,128)} %src_h.1, f32[1,1,16]{2,1,0:T(1,128)} %met_h.1, f32[3,8,8,128]{3,2,1,0:T(8,128)} %bvel_h.1, s32[5,1,128]{2,1,0:T(1,128)} %bitcast.10, f32[15,1,128]{2,1,0:T(1,128)} %bitcast.7, ...), custom_call_target="tpu_custom_call" | custom-call | tf_op jit(solution)/shard_map/pallas_call | solution.py:772
  26.2 0.7 %shard_map.113 = (f32[8,8,128]{2,1,0:T(8,128)}, f32[3,8,8,128]{3,2,1,0:T(8,128)}, f32[15,1,128]{2,1,0:T(1,128)}) custom-call(f32[8,8,128]{2,1,0:T(8,128)S(1)} %get-tuple-element.9.p_in, f32[3,8,8,128]{3,2,1,0:T(8,128)S(1)} %get-tuple-element.10.m_in, f32[15,1,128]{2,1,0:T(1,128)S(1)} %get-tuple-element.11.acc_in), custom_call_target="tpu_custom_call" | custom-call | tf_op jit(solution)/shard_map/pallas_call | solution.py:831

commit v7 on v6

--- a/solution.py
+++ b/solution.py
@@ -204,7 +204,7 @@
                 )
 
     barrier = pltpu.get_barrier_semaphore()
-    partners = FAR_CORNERS + FAR + CORNERS + FACES
+    partners = sorted(FAR_CORNERS + FAR + CORNERS + FACES, key=lambda d: (-abs(d[0]), -abs(d[1])))
     greeted = jnp.int32(0)
     for d in partners:
         there = exists(*d)

time: 27 us -> 27 us (level)
  no operation moved by 1% of the time
where the time goes in v7:
time: 27 us; the launch traced here: 26.8 us
  Pallas kernels  26.2 us (97%)
  between operations  0.64 us (2%)
    pallas_call x1, Pallas kernels, on_device(): pl.pallas_call(kernel, out_shape=shapes, in_specs=[hbm] * 9, out_specs=(v...  25.5 us
    pallas_call x1, Pallas kernels, on_device(): pl.pallas_call(deliver, out_shape=shapes, in_specs=[vmem] * 3, out_specs=...  0.68 us

profile of v7, /device:TPU:7, one launch (start us, length us, event | category | flops | bytes accessed | tf_op | source)
XLA Modules:
  0.0 26.8 jit_solution(9871152692920756773)
XLA Ops:
  0.6 25.5 %shard_map.112 = (f32[8,8,128]{2,1,0:T(8,128)S(1)}, f32[3,8,8,128]{3,2,1,0:T(8,128)S(1)}, f32[15,1,128]{2,1,0:T(1,128)S(1)}) custom-call(f32[8,8,128]{2,1,0:T(8,128)} %src_h.1, f32[1,1,16]{2,1,0:T(1,128)} %met_h.1, f32[3,8,8,128]{3,2,1,0:T(8,128)} %bvel_h.1, s32[5,1,128]{2,1,0:T(1,128)} %bitcast.10, f32[15,1,128]{2,1,0:T(1,128)} %bitcast.7, ...), custom_call_target="tpu_custom_call" | custom-call | tf_op jit(solution)/shard_map/pallas_call | solution.py:772
  26.2 0.7 %shard_map.113 = (f32[8,8,128]{2,1,0:T(8,128)}, f32[3,8,8,128]{3,2,1,0:T(8,128)}, f32[15,1,128]{2,1,0:T(1,128)}) custom-call(f32[8,8,128]{2,1,0:T(8,128)S(1)} %get-tuple-element.9.p_in, f32[3,8,8,128]{3,2,1,0:T(8,128)S(1)} %get-tuple-element.10.m_in, f32[15,1,128]{2,1,0:T(1,128)S(1)} %get-tuple-element.11.acc_in), custom_call_target="tpu_custom_call" | custom-call | tf_op jit(solution)/shard_map/pallas_call | solution.py:831
